TPU v7x, 32 devices: a whole 2x2x4 slice. The times are simulated.
32 devices in a mesh: survey: 2 (over y), band: 4 (over z), role: 4 (over x, core).
Axes of the slice: x: 2, y: 2, z: 4, core: 2. Of those that a mesh axis runs over, the one named last changes fastest.
Arguments:
- vel_index: int32 [16, 32, 128], P('role', 'band'), may hold values from 0 to 31
- courant: float32 [32], replicated, may hold values from 0.05 to 0.19
- src_now: float32 [32, 32, 128], P(('survey', 'role'), 'band'), parts along dimension 0, may hold values from -4 to 4
- src_prev: float32 [32, 32, 128], P(('survey', 'role'), 'band'), parts along dimension 0, may hold values from -4 to 4
- rec_now: float32 [32, 32, 128], P(('survey', 'role'), 'band'), parts along dimension 0, may hold values from -4 to 4
- rec_prev: float32 [32, 32, 128], P(('survey', 'role'), 'band'), parts along dimension 0, may hold values from -4 to 4
- src_pos: int32 [8, 3], P('survey'), parts along dimension 0, may hold values from 0 to 127, as said below
- src_wavelet: float32 [8, 16], P('survey'), parts along dimension 0, may hold values from -16 to 16
- rec_pos: int32 [8192, 2], P('survey'), parts along dimension 0, may hold values from 0 to 127, as said below
- rec_traces: float32 [8192, 16], P('survey'), parts along dimension 0, may hold values from -16 to 16
- offset_lags: int32 [32], replicated, may hold values from -16 to 16, as said below
Outputs:
- image: bfloat16 [64, 16, 32, 128], P('survey', 'role', 'band'), parts along dimension 0
- src_final: float32 [32, 32, 128], P(('survey', 'role'), 'band'), parts along dimension 0
- rec_final: float32 [32, 32, 128], P(('survey', 'role'), 'band'), parts along dimension 0
There are 2 independent parts, one for each index of `survey`. A program takes and returns all parts, laid end to end along the dimension named above; an argument that names none is the same for every part. Nothing has to cross between parts.
Inputs may be any that keep to these rules, and one draw needn't show every extreme that they name: `src_pos`: column 0 is a depth cell below 16, column 1 a cross-line cell below 32, column 2 an inline cell below 128; sources may share cells. `rec_pos`: column 0 is a cross-line cell below 32, column 1 an inline cell below 128; receivers may share cells. `offset_lags`: increasing and distinct: every whole number from -16 to 16 except one of the interior ones.
All inputs are finite; a program needn't handle non-finite values.
Results may differ from a plain program's by a relative error of at most 0.004.
Values may be sent and summed in bfloat16 or wider, within the bound.
A program may use at most 128 MiB of HBM per device.

v0:
```python
import jax
import jax.numpy as jnp
from jax import lax
from jax.sharding import PartitionSpec as P

SUB = 4
IMAGES = 4


STENCIL_WEIGHTS = (-205.0 / 72.0, 8.0 / 5.0, -1.0 / 5.0, 8.0 / 315.0, -1.0 / 560.0)


def padded_2(block, sides, width):
    for axis, dim in sides:
        count = lax.axis_size(axis)
        forward = [(i, i + 1) for i in range(count - 1)]
        backward = [(target, source) for source, target in forward]
        low = lax.ppermute(
            lax.slice_in_dim(block, block.shape[dim] - width, None, axis=dim), axis, forward
        )
        high = lax.ppermute(lax.slice_in_dim(block, 0, width, axis=dim), axis, backward)
        block = jnp.concatenate([low, block, high], axis=dim)
    return block


def laplace(padded, depth_cells, row_cells, col_cells):

    def window(along_z, along_y, along_x):
        return padded[
            :,
            4 + along_z : 4 + along_z + depth_cells,
            4 + along_y : 4 + along_y + row_cells,
            4 + along_x : 4 + along_x + col_cells,
        ]

    summed = 3.0 * STENCIL_WEIGHTS[0] * window(0, 0, 0)
    for distance in range(1, 5):
        weight = STENCIL_WEIGHTS[distance]
        pairs = window(distance, 0, 0) + window(-distance, 0, 0)
        pairs = pairs + window(0, distance, 0) + window(0, -distance, 0)
        pairs = pairs + window(0, 0, distance) + window(0, 0, -distance)
        summed = summed + weight * pairs
    return summed


def lookup(vel_index, courant):
    levels = courant.shape[0]

    def add_level(level, summed):
        return summed + jnp.where(vel_index == level, courant[level], 0.0)

    return lax.fori_loop(0, levels, add_level, jnp.zeros(vel_index.shape, jnp.float32))


def local_index(global_at, start, extent):
    local_at = global_at - start
    inside = (local_at >= 0) & (local_at < extent)
    return jnp.where(inside, local_at, extent)


def inject_all(shape, depth_at, row_at, col_at, amounts):
    step_count = amounts.shape[1]
    return (
        jnp.zeros((step_count,) + shape, jnp.float32)
        .at[:, depth_at, row_at, col_at]
        .add(amounts.T, mode="drop")
    )


def lag_products(source_pad, receiver_pad, offset_lags, max_lag, col_cells):

    def product(lag_value):
        src_part = lax.dynamic_slice_in_dim(source_pad, max_lag - lag_value, col_cells, 2)
        rec_part = lax.dynamic_slice_in_dim(receiver_pad, max_lag + lag_value, col_cells, 2)
        return src_part * rec_part

    return jax.vmap(product)(offset_lags)


def depth_filter(padded, depth_cells):
    return (
        2.0 * padded[:, 1 : 1 + depth_cells]
        - padded[:, 0:depth_cells]
        - padded[:, 2 : 2 + depth_cells]
    )


def pad_inline(state, max_lag):
    return jnp.pad(state, ((0, 0), (0, 0), (0, 0), (max_lag, max_lag)))


def accumulate(slab_state, image_sum, edge_sum, offset_lags, max_lag):
    col_cells = slab_state.shape[3]
    padded = pad_inline(slab_state, max_lag)
    image_sum = image_sum + lag_products(padded[0], padded[1], offset_lags, max_lag, col_cells)
    return (image_sum, edge_sum)


def finish(image_sum):
    padded = padded_2(image_sum, (("role", 1),), 1)
    return depth_filter(padded, image_sum.shape[1]).astype(jnp.bfloat16)


def shards(
    vel_index,
    courant,
    src_now,
    src_prev,
    rec_now,
    rec_prev,
    src_pos,
    src_wavelet,
    rec_pos,
    rec_traces,
    offset_lags,
):
    lag_count = offset_lags.shape[0]
    max_lag = lag_count // 2
    speed = lookup(vel_index, courant)
    band_start = lax.axis_index("band") * src_now.shape[1]
    role_at = lax.axis_index("role")
    current = jnp.stack([src_now, rec_now])
    previous = jnp.stack([src_prev, rec_prev])
    depth_start = role_at * src_now.shape[0]
    col_start = 0

    def faces(state):
        padded = padded_2(state, (("band", 2), ("role", 1)), 4)
        return jnp.pad(padded, ((0, 0), (0, 0), (0, 0), (4, 4)))

    depth_cells, row_cells, col_cells = speed.shape
    shape = speed.shape
    slab_shape = src_now.shape
    src_depth = local_index(src_pos[:, 0], depth_start, depth_cells)
    src_row = local_index(src_pos[:, 1], band_start, row_cells)
    src_col = local_index(src_pos[:, 2], col_start, col_cells)
    rec_depth = local_index(jnp.zeros_like(rec_pos[:, 0]), depth_start, depth_cells)
    rec_row = local_index(rec_pos[:, 0], band_start, row_cells)
    rec_col = local_index(rec_pos[:, 1], col_start, col_cells)
    src_terms = inject_all(shape, src_depth, src_row, src_col, src_wavelet)
    rec_terms = inject_all(shape, rec_depth, rec_row, rec_col, rec_traces)
    image_sum = jnp.zeros((lag_count,) + slab_shape, jnp.float32)
    edge_sum = jnp.zeros((lag_count, 2) + slab_shape[1:], jnp.float32)
    slab_state = current
    for snapshot in range(IMAGES):

        def advance(substep, carry):
            state, older = carry
            tick_at = snapshot * SUB + substep
            sources = jnp.stack(
                [
                    lax.dynamic_index_in_dim(src_terms, tick_at, 0, keepdims=False),
                    lax.dynamic_index_in_dim(rec_terms, tick_at, 0, keepdims=False),
                ]
            )
            laplacian = laplace(faces(state), depth_cells, row_cells, col_cells)
            updated = 2.0 * state - older + speed * (laplacian + sources)
            return (updated, state)

        current, previous = lax.fori_loop(0, SUB, advance, (current, previous))
        slab_state = current
        image_sum, edge_sum = accumulate(slab_state, image_sum, edge_sum, offset_lags, max_lag)
    image = finish(image_sum)
    return (image, slab_state[0], slab_state[1])


def solution(mesh):
    placed = (
        P("role", "band", None),
        P(),
        P(("survey", "role"), "band", None),
        P(("survey", "role"), "band", None),
        P(("survey", "role"), "band", None),
        P(("survey", "role"), "band", None),
        P("survey", None),
        P("survey", None),
        P("survey", None),
        P("survey", None),
        P(),
    )
    return jax.shard_map(
        shards,
        mesh=mesh,
        in_specs=placed,
        out_specs=(
            P("survey", "role", "band", None),
            P(("survey", "role"), "band", None),
            P(("survey", "role"), "band", None),
        ),
        check_vma=False,
    )
```

profile of v0, /device:TPU:0, one launch (start us, length us, event | category | flops | bytes accessed | tf_op | source)
XLA Modules:
  0.0 502.0 jit_solution(1492529173668572404)
XLA Ops:
  0.7 83.2 %while.86 = (s32[]{:T(128)}, f32[4,8,128]{2,1,0:T(8,128)S(1)}, s32[4,8,128]{2,1,0:T(8,128)}, f32[32]{0:T(128)}, s32[]{:T(128)}, /*index=5*/s32[]{:T(128)}) while((s32[]{:T(128)}, f32[4,8,128]{2,1,0:T(8,128)S(1)}, s32[4,8,128]{2,1,0:T(8,128)}, f32[32]{0:T(128)}, s32[]{:T(128)}, /*index=5*/s32[]{:T(128)}) %tuple.207), condition=%wide.region_3.4_spmd.clone, body=%wide.region_2.3_spmd.clone.sunk | while | flops 16387 | bytes 49259 | solution.py:52
  90.3 23.3 %scatter_custom_fusion.1 = f32[16,4096]{0,1:T(8,128)S(1)} fusion(s32[4096]{0:T(1024)S(1)} %broadcast_select_fusion, f32[4096,16]{1,0:T(8,128)} %copy.49, f32[]{:T(128)} %constant.463.clone.1), kind=kCustom, calls=%fused_computation.247 | custom fusion | flops 65536 | bytes 262656
  116.0 66.6 %while.82 = (s32[]{:T(128)}, f32[2,4,8,128]{3,2,1,0:T(8,128)S(1)}, f32[2,4,8,128]{3,2,1,0:T(8,128)S(1)}, f32[4,8,128]{2,1,0:T(8,128)S(1)}, f32[16,4,8,128]{3,2,1...) while((s32[]{:T(128)}, f32[2,4,8,128]{3,2,1,0:T(8,128)S(1)}, f32[2,4,8,128]{3,2,1,0:T(8,128)S(1)}, ...), condition=%wide.region_5.6_spmd, body=%wide.region_4.5_spmd.sunk | while | flops 1126402 | bytes 2322673 | solution.py:160
  116.0 4.9 collective-permute-start
  182.6 61.8 %while.83 = (s32[]{:T(128)}, f32[2,4,8,128]{3,2,1,0:T(8,128)S(1)}, f32[2,4,8,128]{3,2,1,0:T(8,128)S(1)}, f32[4,8,128]{2,1,0:T(8,128)S(1)}, f32[16,4,8,128]{3,2,1...) while((s32[]{:T(128)}, f32[2,4,8,128]{3,2,1,0:T(8,128)S(1)}, ...), condition=%wide.region_7.8_spmd, body=%wide.region_6.7_spmd.sunk | while | flops 1126406 | bytes 2322743 | solution.py:160
  244.4 61.8 %while.84 = (s32[]{:T(128)}, f32[2,4,8,128]{3,2,1,0:T(8,128)S(1)}, f32[2,4,8,128]{3,2,1,0:T(8,128)S(1)}, f32[4,8,128]{2,1,0:T(8,128)S(1)}, f32[16,4,8,128]{3,2,1...) while((s32[]{:T(128)}, f32[2,4,8,128]{3,2,1,0:T(8,128)S(1)}, ...), condition=%wide.region_9.10_spmd, body=%wide.region_8.9_spmd.sunk | while | flops 1126406 | bytes 2322743 | solution.py:160
  308.4 61.8 %while.85 = (s32[]{:T(128)}, f32[2,4,8,128]{3,2,1,0:T(8,128)S(1)}, f32[2,4,8,128]{3,2,1,0:T(8,128)S(1)}, f32[4,8,128]{2,1,0:T(8,128)S(1)}, f32[16,4,8,128]{3,2,1...) while((s32[]{:T(128)}, f32[2,4,8,128]{3,2,1,0:T(8,128)S(1)}, ...), condition=%wide.region_11.12_spmd, body=%wide.region_10.11_spmd.sunk | while | flops 1126406 | bytes 2322743 | solution.py:160
  372.1 7.9 %gather_fusion.1 = f32[32,4,8,128]{2,1,3,0:T(4,128)} fusion(f32[4,8,160]{1,0,2:T(4,128)S(1)} %get-tuple-element.879, s32[32]{0:T(128)S(1)} %get-tuple-element.891), kind=kCustom, calls=%fused_computation.1 | custom fusion | bytes 1048960 | tf_op jit(solution)/shard_map/vmap()/gather | solution.py:74
  379.9 6.6 %copy.54 = f32[32,4,8,128]{3,2,1,0:T(8,128)S(1)} copy(f32[32,4,8,128]{2,1,3,0:T(4,128)} %gather_fusion.1) | data formatting | bytes 1048576 | tf_op jit(solution)/shard_map/vmap()/gather | solution.py:74
  386.5 7.9 %gather_fusion.3 = f32[32,4,8,128]{2,1,3,0:T(4,128)} fusion(f32[4,8,160]{1,0,2:T(4,128)S(1)} %get-tuple-element.881, s32[32]{0:T(128)S(1)} %get-tuple-element.891), kind=kCustom, calls=%fused_computation.3 | custom fusion | bytes 1048960 | tf_op jit(solution)/shard_map/vmap()/gather | solution.py:74
  394.4 6.6 %copy.59 = f32[32,4,8,128]{3,2,1,0:T(8,128)S(1)} copy(f32[32,4,8,128]{2,1,3,0:T(4,128)} %gather_fusion.3) | data formatting | bytes 1048576 | tf_op jit(solution)/shard_map/vmap()/gather | solution.py:74
  401.0 8.1 %gather_fusion.5 = f32[32,4,8,128]{2,1,3,0:T(4,128)} fusion(f32[4,8,160]{1,0,2:T(4,128)S(1)} %get-tuple-element.883, s32[32]{0:T(128)S(1)} %get-tuple-element.891), kind=kCustom, calls=%fused_computation.5 | custom fusion | bytes 1048960 | tf_op jit(solution)/shard_map/vmap()/gather | solution.py:74
  409.0 6.6 %copy.64 = f32[32,4,8,128]{3,2,1,0:T(8,128)S(1)} copy(f32[32,4,8,128]{2,1,3,0:T(4,128)} %gather_fusion.5) | data formatting | bytes 1048576 | tf_op jit(solution)/shard_map/vmap()/gather | solution.py:74
  415.6 7.9 %gather_fusion.7 = f32[32,4,8,128]{2,1,3,0:T(4,128)} fusion(f32[4,8,160]{1,0,2:T(4,128)S(1)} %get-tuple-element.885, s32[32]{0:T(128)S(1)} %get-tuple-element.891), kind=kCustom, calls=%fused_computation.7 | custom fusion | bytes 1048960 | tf_op jit(solution)/shard_map/vmap()/gather | solution.py:74
  423.5 7.4 %copy.69 = f32[32,4,8,128]{3,2,1,0:T(8,128)} copy(f32[32,4,8,128]{2,1,3,0:T(4,128)} %gather_fusion.7) | data formatting | bytes 1048576 | tf_op jit(solution)/shard_map/vmap()/gather | solution.py:74
  430.9 7.9 %gather_fusion = f32[32,4,8,128]{2,1,3,0:T(4,128)} fusion(f32[4,8,160]{1,0,2:T(4,128)S(1)} %get-tuple-element.880, s32[32]{0:T(128)S(1)} %get-tuple-element.892), kind=kCustom, calls=%fused_computation | custom fusion | bytes 1048960 | tf_op jit(solution)/shard_map/vmap()/gather | solution.py:73
  438.7 6.6 %copy.53 = f32[32,4,8,128]{3,2,1,0:T(8,128)S(1)} copy(f32[32,4,8,128]{2,1,3,0:T(4,128)} %gather_fusion) | data formatting | bytes 1048576 | tf_op jit(solution)/shard_map/vmap()/gather | solution.py:73
  445.3 7.9 %gather_fusion.2 = f32[32,4,8,128]{2,1,3,0:T(4,128)} fusion(f32[4,8,160]{1,0,2:T(4,128)S(1)} %get-tuple-element.882, s32[32]{0:T(128)S(1)} %get-tuple-element.892), kind=kCustom, calls=%fused_computation.2 | custom fusion | bytes 1048960 | tf_op jit(solution)/shard_map/vmap()/gather | solution.py:73
  453.2 7.4 %copy.58 = f32[32,4,8,128]{3,2,1,0:T(8,128)} copy(f32[32,4,8,128]{2,1,3,0:T(4,128)} %gather_fusion.2) | data formatting | bytes 1048576 | tf_op jit(solution)/shard_map/vmap()/gather | solution.py:73
  460.5 8.1 %gather_fusion.4 = f32[32,4,8,128]{2,1,3,0:T(4,128)} fusion(f32[4,8,160]{1,0,2:T(4,128)S(1)} %get-tuple-element.884, s32[32]{0:T(128)S(1)} %get-tuple-element.892), kind=kCustom, calls=%fused_computation.4 | custom fusion | bytes 1048960 | tf_op jit(solution)/shard_map/vmap()/gather | solution.py:73
  468.6 7.4 %copy.63 = f32[32,4,8,128]{3,2,1,0:T(8,128)} copy(f32[32,4,8,128]{2,1,3,0:T(4,128)} %gather_fusion.4) | data formatting | bytes 1048576 | tf_op jit(solution)/shard_map/vmap()/gather | solution.py:73
  476.1 7.9 %gather_fusion.6 = f32[32,4,8,128]{2,1,3,0:T(4,128)} fusion(f32[4,8,160]{1,0,2:T(4,128)S(1)} %get-tuple-element.886, s32[32]{0:T(128)S(1)} %get-tuple-element.892), kind=kCustom, calls=%fused_computation.6 | custom fusion | bytes 1048960 | tf_op jit(solution)/shard_map/vmap()/gather | solution.py:73
  483.9 7.4 %copy.68 = f32[32,4,8,128]{3,2,1,0:T(8,128)} copy(f32[32,4,8,128]{2,1,3,0:T(4,128)} %gather_fusion.6) | data formatting | bytes 1048576 | tf_op jit(solution)/shard_map/vmap()/gather | solution.py:73
  493.2 4.8 collective-permute-start.16
  (382 shorter events, 346.9 us)
Async XLA Ops:
  116.0 6.4 %collective-permute-start = (f32[2,4,4,128]{3,2,1,0:T(4,128)S(1)}, f32[2,4,4,128]{3,2,1,0:T(4,128)S(1)}, u32[]{:S(2)}, u32[]{:S(2)}) collective-permute-start(f32[2,4,4,128]{3,2,1,0:T(4,128)S(1)} %get-tuple-element.1062), channel_id=1, source_target_pairs={{0,4},{4,8},{8,12},{1,5},{5,9},{9,13},{2,6},{6,10},{10,14},{3,7},{... | collective-permute-start | bytes 49160 | tf_op jit(solution)/shard_map/while/body/eval_jaxpr/ppermute | solution.py:18
  120.9 5.6 %collective-permute-start.1 = (f32[2,4,4,128]{3,2,1,0:T(4,128)S(1)}, f32[2,4,4,128]{3,2,1,0:T(4,128)S(1)}, u32[]{:S(2)}, u32[]{:S(2)}) collective-permute-start(f32[2,4,4,128]{3,2,1,0:T(4,128)S(1)} %get-tuple-element.1063), channel_id=1, source_target_pairs={{4,0},{8,4},{12,8},{5,1},{9,5},{13,9},{6,2},{10,6},{14,10},{7,3},{... | collective-permute-start | bytes 49160 | tf_op jit(solution)/shard_map/while/body/eval_jaxpr/ppermute | solution.py:21
  127.9 4.9 collective-permute-start.2
  133.2 4.9 collective-permute-start
  136.6 5.6 %collective-permute-start.1 = (f32[2,4,4,128]{3,2,1,0:T(4,128)S(1)}, f32[2,4,4,128]{3,2,1,0:T(4,128)S(1)}, u32[]{:S(2)}, u32[]{:S(2)}) collective-permute-start(f32[2,4,4,128]{3,2,1,0:T(4,128)S(1)} %get-tuple-element.1063), channel_id=1, source_target_pairs={{4,0},{8,4},{12,8},{5,1},{9,5},{13,9},{6,2},{10,6},{14,10},{7,3},{... | collective-permute-start | bytes 49160 | tf_op jit(solution)/shard_map/while/body/eval_jaxpr/ppermute | solution.py:21
  142.3 4.7 collective-permute-start.3
  150.2 4.9 collective-permute-start
  153.7 5.6 %collective-permute-start.1 = (f32[2,4,4,128]{3,2,1,0:T(4,128)S(1)}, f32[2,4,4,128]{3,2,1,0:T(4,128)S(1)}, u32[]{:S(2)}, u32[]{:S(2)}) collective-permute-start(f32[2,4,4,128]{3,2,1,0:T(4,128)S(1)} %get-tuple-element.1063), channel_id=1, source_target_pairs={{4,0},{8,4},{12,8},{5,1},{9,5},{13,9},{6,2},{10,6},{14,10},{7,3},{... | collective-permute-start | bytes 49160 | tf_op jit(solution)/shard_map/while/body/eval_jaxpr/ppermute | solution.py:21
  159.3 4.7 collective-permute-start.3
  169.1 5.6 %collective-permute-start.1 = (f32[2,4,4,128]{3,2,1,0:T(4,128)S(1)}, f32[2,4,4,128]{3,2,1,0:T(4,128)S(1)}, u32[]{:S(2)}, u32[]{:S(2)}) collective-permute-start(f32[2,4,4,128]{3,2,1,0:T(4,128)S(1)} %get-tuple-element.1063), channel_id=1, source_target_pairs={{4,0},{8,4},{12,8},{5,1},{9,5},{13,9},{6,2},{10,6},{14,10},{7,3},{... | collective-permute-start | bytes 49160 | tf_op jit(solution)/shard_map/while/body/eval_jaxpr/ppermute | solution.py:21
  184.6 5.6 %collective-permute-start.5 = (f32[2,4,4,128]{3,2,1,0:T(4,128)S(1)}, f32[2,4,4,128]{3,2,1,0:T(4,128)S(1)}, u32[]{:S(2)}, u32[]{:S(2)}) collective-permute-start(f32[2,4,4,128]{3,2,1,0:T(4,128)S(1)} %get-tuple-element.1073), channel_id=1, source_target_pairs={{4,0},{8,4},{12,8},{5,1},{9,5},{13,9},{6,2},{10,6},{14,10},{7,3},{... | collective-permute-start | bytes 49160 | tf_op jit(solution)/shard_map/while/body/eval_jaxpr/ppermute | solution.py:21
  200.0 5.6 %collective-permute-start.5 = (f32[2,4,4,128]{3,2,1,0:T(4,128)S(1)}, f32[2,4,4,128]{3,2,1,0:T(4,128)S(1)}, u32[]{:S(2)}, u32[]{:S(2)}) collective-permute-start(f32[2,4,4,128]{3,2,1,0:T(4,128)S(1)} %get-tuple-element.1073), channel_id=1, source_target_pairs={{4,0},{8,4},{12,8},{5,1},{9,5},{13,9},{6,2},{10,6},{14,10},{7,3},{... | collective-permute-start | bytes 49160 | tf_op jit(solution)/shard_map/while/body/eval_jaxpr/ppermute | solution.py:21
  215.5 5.6 %collective-permute-start.5 = (f32[2,4,4,128]{3,2,1,0:T(4,128)S(1)}, f32[2,4,4,128]{3,2,1,0:T(4,128)S(1)}, u32[]{:S(2)}, u32[]{:S(2)}) collective-permute-start(f32[2,4,4,128]{3,2,1,0:T(4,128)S(1)} %get-tuple-element.1073), channel_id=1, source_target_pairs={{4,0},{8,4},{12,8},{5,1},{9,5},{13,9},{6,2},{10,6},{14,10},{7,3},{... | collective-permute-start | bytes 49160 | tf_op jit(solution)/shard_map/while/body/eval_jaxpr/ppermute | solution.py:21
  230.9 5.6 %collective-permute-start.5 = (f32[2,4,4,128]{3,2,1,0:T(4,128)S(1)}, f32[2,4,4,128]{3,2,1,0:T(4,128)S(1)}, u32[]{:S(2)}, u32[]{:S(2)}) collective-permute-start(f32[2,4,4,128]{3,2,1,0:T(4,128)S(1)} %get-tuple-element.1073), channel_id=1, source_target_pairs={{4,0},{8,4},{12,8},{5,1},{9,5},{13,9},{6,2},{10,6},{14,10},{7,3},{... | collective-permute-start | bytes 49160 | tf_op jit(solution)/shard_map/while/body/eval_jaxpr/ppermute | solution.py:21
  236.6 4.7 collective-permute-start.7
  246.4 5.6 %collective-permute-start.9 = (f32[2,4,4,128]{3,2,1,0:T(4,128)S(1)}, f32[2,4,4,128]{3,2,1,0:T(4,128)S(1)}, u32[]{:S(2)}, u32[]{:S(2)}) collective-permute-start(f32[2,4,4,128]{3,2,1,0:T(4,128)S(1)} %get-tuple-element.1083), channel_id=1, source_target_pairs={{4,0},{8,4},{12,8},{5,1},{9,5},{13,9},{6,2},{10,6},{14,10},{7,3},{... | collective-permute-start | bytes 49160 | tf_op jit(solution)/shard_map/while/body/eval_jaxpr/ppermute | solution.py:21
  261.8 5.6 %collective-permute-start.9 = (f32[2,4,4,128]{3,2,1,0:T(4,128)S(1)}, f32[2,4,4,128]{3,2,1,0:T(4,128)S(1)}, u32[]{:S(2)}, u32[]{:S(2)}) collective-permute-start(f32[2,4,4,128]{3,2,1,0:T(4,128)S(1)} %get-tuple-element.1083), channel_id=1, source_target_pairs={{4,0},{8,4},{12,8},{5,1},{9,5},{13,9},{6,2},{10,6},{14,10},{7,3},{... | collective-permute-start | bytes 49160 | tf_op jit(solution)/shard_map/while/body/eval_jaxpr/ppermute | solution.py:21
  277.3 5.6 %collective-permute-start.9 = (f32[2,4,4,128]{3,2,1,0:T(4,128)S(1)}, f32[2,4,4,128]{3,2,1,0:T(4,128)S(1)}, u32[]{:S(2)}, u32[]{:S(2)}) collective-permute-start(f32[2,4,4,128]{3,2,1,0:T(4,128)S(1)} %get-tuple-element.1083), channel_id=1, source_target_pairs={{4,0},{8,4},{12,8},{5,1},{9,5},{13,9},{6,2},{10,6},{14,10},{7,3},{... | collective-permute-start | bytes 49160 | tf_op jit(solution)/shard_map/while/body/eval_jaxpr/ppermute | solution.py:21
  292.7 5.6 %collective-permute-start.9 = (f32[2,4,4,128]{3,2,1,0:T(4,128)S(1)}, f32[2,4,4,128]{3,2,1,0:T(4,128)S(1)}, u32[]{:S(2)}, u32[]{:S(2)}) collective-permute-start(f32[2,4,4,128]{3,2,1,0:T(4,128)S(1)} %get-tuple-element.1083), channel_id=1, source_target_pairs={{4,0},{8,4},{12,8},{5,1},{9,5},{13,9},{6,2},{10,6},{14,10},{7,3},{... | collective-permute-start | bytes 49160 | tf_op jit(solution)/shard_map/while/body/eval_jaxpr/ppermute | solution.py:21
  310.4 5.6 %collective-permute-start.13 = (f32[2,4,4,128]{3,2,1,0:T(4,128)S(1)}, f32[2,4,4,128]{3,2,1,0:T(4,128)S(1)}, u32[]{:S(2)}, u32[]{:S(2)}) collective-permute-start(f32[2,4,4,128]{3,2,1,0:T(4,128)S(1)} %get-tuple-element.1093), channel_id=1, source_target_pairs={{4,0},{8,4},{12,8},{5,1},{9,5},{13,9},{6,2},{10,6},{14,10},{7,3},{... | collective-permute-start | bytes 49160 | tf_op jit(solution)/shard_map/while/body/eval_jaxpr/ppermute | solution.py:21
  325.8 5.6 %collective-permute-start.13 = (f32[2,4,4,128]{3,2,1,0:T(4,128)S(1)}, f32[2,4,4,128]{3,2,1,0:T(4,128)S(1)}, u32[]{:S(2)}, u32[]{:S(2)}) collective-permute-start(f32[2,4,4,128]{3,2,1,0:T(4,128)S(1)} %get-tuple-element.1093), channel_id=1, source_target_pairs={{4,0},{8,4},{12,8},{5,1},{9,5},{13,9},{6,2},{10,6},{14,10},{7,3},{... | collective-permute-start | bytes 49160 | tf_op jit(solution)/shard_map/while/body/eval_jaxpr/ppermute | solution.py:21
  341.3 5.6 %collective-permute-start.13 = (f32[2,4,4,128]{3,2,1,0:T(4,128)S(1)}, f32[2,4,4,128]{3,2,1,0:T(4,128)S(1)}, u32[]{:S(2)}, u32[]{:S(2)}) collective-permute-start(f32[2,4,4,128]{3,2,1,0:T(4,128)S(1)} %get-tuple-element.1093), channel_id=1, source_target_pairs={{4,0},{8,4},{12,8},{5,1},{9,5},{13,9},{6,2},{10,6},{14,10},{7,3},{... | collective-permute-start | bytes 49160 | tf_op jit(solution)/shard_map/while/body/eval_jaxpr/ppermute | solution.py:21
  356.7 5.6 %collective-permute-start.13 = (f32[2,4,4,128]{3,2,1,0:T(4,128)S(1)}, f32[2,4,4,128]{3,2,1,0:T(4,128)S(1)}, u32[]{:S(2)}, u32[]{:S(2)}) collective-permute-start(f32[2,4,4,128]{3,2,1,0:T(4,128)S(1)} %get-tuple-element.1093), channel_id=1, source_target_pairs={{4,0},{8,4},{12,8},{5,1},{9,5},{13,9},{6,2},{10,6},{14,10},{7,3},{... | collective-permute-start | bytes 49160 | tf_op jit(solution)/shard_map/while/body/eval_jaxpr/ppermute | solution.py:21
  493.2 6.8 %collective-permute-start.16 = (f32[32,1,8,128]{3,2,1,0:T(8,128)S(1)}, f32[32,1,8,128]{3,2,1,0:T(8,128)S(1)}, u32[]{:S(2)}, u32[]{:S(2)}) collective-permute-start(f32[32,1,8,128]{3,2,1,0:T(8,128)S(1)} %get-tuple-element.877), channel_id=1, source_target_pairs={{0,1},{1,2},{2,3},{4,5},{5,6},{6,7},{8,9},{9,10},{10,11},{12,13},{... | collective-permute-start | bytes 393224 | tf_op jit(solution)/shard_map/ppermute | solution.py:18
  (50 other events, 893.5 us)
where the time goes:
time: 510 us; the launch traced here: 502 us
  local copies, waits for them, and re-layouts  172 us (34%)
  starting transfers between devices  137 us (27%)
  waiting for transfers between devices  112 us (22%)
  other arithmetic  78.5 us (15%)
    ppermute x33, waiting for transfers between devices, padded_2(): lax.ppermute(lax.slice_in_dim(block, 0, width, axis=dim), axis, backward)  110 us
    ppermute x33, starting transfers between devices, padded_2(): lax.ppermute(lax.slice_in_dim(block, block.shape[dim] - width, None, axis...  94.2 us
    gather x8, local copies, waits for them, and re-layouts, product(): lax.dynamic_slice_in_dim(source_pad, max_lag - lag_value, col_cells, 2)  60.4 us
    gather x8, local copies, waits for them, and re-layouts, product(): lax.dynamic_slice_in_dim(receiver_pad, max_lag + lag_value, col_cells, 2)  58.8 us
    ppermute x33, starting transfers between devices, padded_2(): lax.ppermute(lax.slice_in_dim(block, 0, width, axis=dim), axis, backward)  42.6 us
    add x32, other arithmetic, add_level(): return summed + jnp.where(vel_index == level, courant[level], 0.0)  42.5 us
    dynamic_slice x32, local copies, waits for them, and re-layouts, add_level(): return summed + jnp.where(vel_index == level, courant[level], 0.0)  40.6 us
    unnamed x5, other arithmetic  24.9 us
  transfers between devices with their start and end apart: 66, of which 45 were waited for; matrix products, arithmetic and copies ran while one was open for 1% of the time, Pallas kernels for 0%

commit v1 on v0

--- a/solution.py
+++ b/solution.py
@@ -1,10 +1,18 @@
+import functools
+
 import jax
 import jax.numpy as jnp
 from jax import lax
+from jax.experimental import pallas as pl
+from jax.experimental.pallas import tpu as pltpu
 from jax.sharding import PartitionSpec as P
 
 SUB = 4
 IMAGES = 4
+HALO = 4
+WINDOW_CELLS = 1 << 17
+MESH = pl.DeviceIdType.MESH
+WIRE = jnp.bfloat16
 
 
 STENCIL_WEIGHTS = (-205.0 / 72.0, 8.0 / 5.0, -1.0 / 5.0, 8.0 / 315.0, -1.0 / 560.0)
@@ -101,7 +109,7 @@
     return depth_filter(padded, image_sum.shape[1]).astype(jnp.bfloat16)
 
 
-def shards(
+def tile_shards(
     vel_index,
     courant,
     src_now,
@@ -164,6 +172,407 @@
     return (image, slab_state[0], slab_state[1])
 
 
+def split_two(value):
+    high = value.astype(jnp.bfloat16)
+    low = (value - high.astype(jnp.float32)).astype(jnp.bfloat16)
+    return high, low
+
+
+def inline_matrix(cols):
+    row = lax.broadcasted_iota(jnp.int32, (cols, cols), 0)
+    col = lax.broadcasted_iota(jnp.int32, (cols, cols), 1)
+    apart = jnp.abs(row - col)
+    matrix = jnp.where(apart == 0, 3.0 * STENCIL_WEIGHTS[0], 0.0)
+    for distance in range(1, 5):
+        matrix = jnp.where(apart == distance, STENCIL_WEIGHTS[distance], matrix)
+    return matrix
+
+
+def window_kernel(
+    bands,
+    roles,
+    vel_ref,
+    courant_ref,
+    src_now_ref,
+    src_prev_ref,
+    rec_now_ref,
+    rec_prev_ref,
+    src_pos_ref,
+    src_wave_ref,
+    rec_pos_ref,
+    rec_trace_ref,
+    lags_ref,
+    image_ref,
+    src_out_ref,
+    rec_out_ref,
+    out_buf,
+    blocks,
+    field_a,
+    field_b,
+    speed_ref,
+    split_ref,
+    inline_ref,
+    base_ref,
+    inject_ref,
+    stage_ref,
+    snap_ref,
+    near_send,
+    far_send,
+    block_recv,
+    snap_send,
+    snap_recv,
+):
+    depth, rows, cols = vel_ref.shape
+    full_z, full_y = depth * roles, rows * bands
+    cells = depth * rows
+    columns = roles // 2
+    survey = lax.axis_index("survey")
+    band = lax.axis_index("band")
+    role = lax.axis_index("role")
+    core = lax.rem(role, 2)
+    column = role // 2
+    own = band * roles + role
+    f32 = jnp.float32
+    y0 = 8
+
+    def device(at_band, at_role):
+        return (survey, at_band, at_role)
+
+    partner = device(band, 2 * column + 1 - core)
+    barrier = pltpu.get_barrier_semaphore()
+    greeted = 0
+    for step in range(1, bands):
+        for side in range(2):
+            pl.semaphore_signal(
+                barrier,
+                inc=1,
+                device_id=device(lax.rem(band + step, bands), 2 * column + side),
+                device_id_type=MESH,
+            )
+            greeted += 1
+    pl.semaphore_signal(barrier, inc=1, device_id=partner, device_id_type=MESH)
+    greeted += 1
+    for step in range(1, columns):
+        pl.semaphore_signal(
+            barrier,
+            inc=1,
+            device_id=device(band, 2 * lax.rem(column + step, columns) + core),
+            device_id_type=MESH,
+        )
+        greeted += 1
+
+    index = vel_ref[...].astype(f32).reshape(cells, cols)
+    for side, now_ref, prev_ref in ((0, src_now_ref, src_prev_ref), (1, rec_now_ref, rec_prev_ref)):
+        now = now_ref[...].reshape(cells, cols)
+        change = now - prev_ref[...].reshape(cells, cols)
+        out_buf[side, 0:cells] = now.astype(WIRE)
+        out_buf[side, cells : 2 * cells] = change.astype(WIRE)
+        out_buf[side, 2 * cells : 3 * cells] = index.astype(WIRE)
+    pl.semaphore_wait(barrier, greeted)
+
+    sends = []
+    for step in range(1, bands):
+        for side in range(2):
+            copy = pltpu.make_async_remote_copy(
+                src_ref=out_buf.at[side],
+                dst_ref=blocks.at[own],
+                send_sem=near_send.at[2 * step + side],
+                recv_sem=block_recv.at[own],
+                device_id=device(lax.rem(band + step, bands), 2 * column + side),
+                device_id_type=MESH,
+            )
+            copy.start()
+            sends.append(copy)
+    copy = pltpu.make_async_remote_copy(
+        src_ref=out_buf.at[1 - core],
+        dst_ref=blocks.at[own],
+        send_sem=near_send.at[0],
+        recv_sem=block_recv.at[own],
+        device_id=partner,
+        device_id_type=MESH,
+    )
+    copy.start()
+    sends.append(copy)
+
+    def pass_on(step, source, slot, lane):
+        copy = pltpu.make_async_remote_copy(
+            src_ref=source,
+            dst_ref=blocks.at[slot],
+            send_sem=far_send.at[lane],
+            recv_sem=block_recv.at[slot],
+            device_id=device(band, 2 * lax.rem(column + step, columns) + core),
+            device_id_type=MESH,
+        )
+        copy.start()
+        sends.append(copy)
+
+    def landed(slot):
+        pltpu.make_async_copy(blocks.at[slot], blocks.at[slot], block_recv.at[slot]).wait()
+
+    for step in range(1, columns):
+        pass_on(step, out_buf.at[core], own, step)
+
+    inject_ref[...] = jnp.zeros_like(inject_ref)
+    lines = split_ref.shape[0]
+    half = cols // 2
+    row_at = lax.broadcasted_iota(jnp.int32, (lines, cols), 0)
+    lane_at = lax.broadcasted_iota(jnp.int32, (lines, cols), 1)
+    lane_low = jnp.where(lane_at >= half, lane_at - half, lane_at)
+    steps = inject_ref.shape[0]
+
+    @pl.when(core == 0)
+    def _():
+        count = src_pos_ref.shape[0]
+        target = jnp.full((1, cols), -1, jnp.int32)
+        lane = lax.broadcasted_iota(jnp.int32, (1, cols), 1)
+        lane = jnp.where(lane >= half, lane - half, lane)
+        for source in range(count):
+            line = src_pos_ref[source, 0] * full_y + src_pos_ref[source, 1]
+            target = jnp.where(lane == source, line, target)
+        split_ref[:, 2 * cols : 3 * cols] = jnp.where(row_at == target, 1.0, 0.0).astype(jnp.bfloat16)
+        height = -(-count // 16) * 16
+        row = lax.broadcasted_iota(jnp.int32, (height, cols), 0)
+        col = lax.broadcasted_iota(jnp.int32, (height, cols), 1)
+        for tick in range(steps):
+            term = jnp.zeros((height, cols), f32)
+            for source in range(count):
+                here = (row == source) & (col == src_pos_ref[source, 2])
+                term = jnp.where(here, src_wave_ref[source, tick], term)
+            high, low = split_two(term)
+            inject_ref[tick, 0:height] = high
+            inject_ref[tick, half : half + height] = low
+
+    @pl.when(core == 1)
+    def _():
+        split_ref[:, 2 * cols : 3 * cols] = jnp.where(
+            (row_at < full_y) & (row_at == lane_low), 1.0, 0.0
+        ).astype(jnp.bfloat16)
+        count = rec_pos_ref.shape[1]
+        chunk = min(512, count)
+        total = jnp.zeros((2 * steps * full_y, cols), f32)
+        for at in range(0, count, chunk):
+            size = min(chunk, count - at)
+            y_at = rec_pos_ref[0:1, at : at + size]
+            x_at = rec_pos_ref[1:2, at : at + size]
+            in_row = lax.broadcasted_iota(jnp.int32, (full_y, size), 0) == y_at
+            in_col = lax.broadcasted_iota(jnp.int32, (cols, size), 0) == x_at
+            in_col = jnp.where(in_col, 1.0, 0.0).astype(jnp.bfloat16)
+            amounts = rec_trace_ref[:, at : at + size]
+            high = amounts.astype(jnp.bfloat16).astype(f32)
+            parts = []
+            for part in (high, amounts - high):
+                for tick in range(steps):
+                    parts.append(jnp.where(in_row, part[tick : tick + 1], 0.0).astype(jnp.bfloat16))
+            total = total + lax.dot_general(
+                jnp.concatenate(parts, axis=0),
+                in_col,
+                (((1,), (1,)), ((), ())),
+                preferred_element_type=f32,
+            )
+        size = steps * full_y
+        high, low = split_two(total[0:size] + total[size : 2 * size])
+        for tick in range(steps):
+            inject_ref[tick, 0:full_y] = high[tick * full_y : (tick + 1) * full_y]
+            inject_ref[tick, half : half + full_y] = low[tick * full_y : (tick + 1) * full_y]
+
+    high, low = split_two(inline_matrix(cols))
+    base_ref[0:cols] = high
+    base_ref[cols : 2 * cols] = high
+    base_ref[2 * cols : 3 * cols] = low
+    field_a[...] = jnp.zeros_like(field_a)
+    field_b[...] = jnp.zeros_like(field_b)
+
+    slot = band * roles + 2 * column + 1 - core
+    landed(slot)
+    for step in range(1, columns):
+        pass_on(step, blocks.at[slot], slot, columns + step)
+    for hop in range(1, bands):
+        for side in range(2):
+            slot = lax.rem(band + hop, bands) * roles + 2 * column + side
+            landed(slot)
+            for step in range(1, columns):
+                pass_on(step, blocks.at[slot], slot, (2 * hop + side) * columns + step)
+    for step in range(1, columns):
+        other = lax.rem(column + step, columns)
+        for at_band in range(bands):
+            for side in range(2):
+                landed(at_band * roles + 2 * other + side)
+    blocks[own] = out_buf[core]
+
+    def table(values):
+        found = jnp.zeros(values.shape, f32)
+        for level in range(courant_ref.shape[0]):
+            found = jnp.where(values == float(level), courant_ref[level], found)
+        return found
+
+    for at_role in range(roles):
+        for at_band in range(bands):
+            block = blocks[at_band * roles + at_role].astype(f32)
+            now = block[0:cells].reshape(depth, rows, cols)
+            prev = now - block[cells : 2 * cells].reshape(depth, rows, cols)
+            z_part = pl.ds(HALO + depth * at_role, depth)
+            y_part = pl.ds(y0 + rows * at_band, rows)
+            field_a[z_part, y_part, :] = now
+            field_b[z_part, y_part, :] = prev
+            speed_ref[pl.ds(depth * at_role, depth), pl.ds(rows * at_band, rows), :] = table(
+                block[2 * cells : 3 * cells]
+            ).reshape(depth, rows, cols)
+
+    own_z = pl.ds(HALO + depth * role, depth)
+    own_y = pl.ds(pl.multiple_of(y0 + rows * band, rows), rows)
+    field_a[own_z, own_y, :] = jnp.where(core == 0, src_now_ref[...], rec_now_ref[...])
+    field_b[own_z, own_y, :] = jnp.where(core == 0, src_prev_ref[...], rec_prev_ref[...])
+
+    def store_split(z_at, value):
+        high, low = split_two(value)
+        split_ref[pl.ds(z_at * full_y, full_y), 0:cols] = low
+        split_ref[pl.ds(z_at * full_y, full_y), cols : 2 * cols] = high
+
+    for z_at in range(full_z):
+        store_split(z_at, field_a[HALO + z_at, y0 : y0 + full_y, :])
+
+    def advance(tick, state, older):
+        weights = jnp.concatenate([base_ref[2 * cols : 3 * cols], inject_ref[tick]], axis=0)
+        inline_ref[...] = jnp.dot(
+            split_ref[:, 0 : 2 * cols], base_ref[0 : 2 * cols], preferred_element_type=f32
+        ) + jnp.dot(split_ref[:, cols : 3 * cols], weights, preferred_element_type=f32)
+        for z_at in range(full_z):
+            total = inline_ref[z_at * full_y : (z_at + 1) * full_y]
+            z_in = HALO + z_at
+            centre = state[z_in, y0 : y0 + full_y, :]
+            for distance in range(1, 5):
+                pairs = state[z_in - distance, y0 : y0 + full_y, :] + state[z_in + distance, y0 : y0 + full_y, :]
+                pairs = pairs + (
+                    state[z_in, y0 - distance : y0 - distance + full_y, :]
+                    + state[z_in, y0 + distance : y0 + distance + full_y, :]
+                )
+                total = total + STENCIL_WEIGHTS[distance] * pairs
+            updated = (2.0 * centre - older[z_in, y0 : y0 + full_y, :]) + speed_ref[z_at] * total
+            older[z_in, y0 : y0 + full_y, :] = updated
+            store_split(z_at, updated)
+
+    partner_role = 2 * column + 1 - core
+    deep = depth + 2
+
+    def snap_copy(snapshot):
+        return pltpu.make_async_remote_copy(
+            src_ref=stage_ref.at[snapshot],
+            dst_ref=snap_ref.at[snapshot, core],
+            send_sem=snap_send.at[snapshot],
+            recv_sem=snap_recv.at[snapshot],
+            device_id=partner,
+            device_id_type=MESH,
+        )
+
+    def one_image(snapshot, carry):
+        for pair in range(SUB // 2):
+            advance(SUB * snapshot + 2 * pair, field_a, field_b)
+            advance(SUB * snapshot + 2 * pair + 1, field_b, field_a)
+        stage_ref[snapshot] = field_a[pl.ds(HALO - 1 + depth * partner_role, deep), own_y, :]
+        snap_copy(snapshot).start()
+        snap_ref[snapshot, core] = field_a[pl.ds(HALO - 1 + depth * role, deep), own_y, :]
+        return carry
+
+    lax.fori_loop(0, IMAGES, one_image, 0)
+    for snapshot in range(IMAGES):
+        snap_copy(snapshot).wait()
+    src_out_ref[...] = snap_ref[IMAGES - 1, 0, 1 : 1 + depth]
+    rec_out_ref[...] = snap_ref[IMAGES - 1, 1, 1 : 1 + depth]
+
+    def one_lag(slot, carry):
+        lag = lags_ref[slot]
+        back = jnp.where(lag > 0, cols - 2 * lag, -2 * lag)
+        shift = jnp.where(lag < 0, cols + lag, lag)
+        summed = jnp.zeros((deep * rows, cols), f32)
+        for snapshot in range(IMAGES):
+            moved = pltpu.roll(snap_ref[snapshot, 1].reshape(deep * rows, cols), back, 1)
+            summed = summed + snap_ref[snapshot, 0].reshape(deep * rows, cols) * moved
+        filtered = (
+            2.0 * summed[rows : rows + cells] - summed[0:cells] - summed[2 * rows : 2 * rows + cells]
+        )
+        filtered = pltpu.roll(filtered, shift, 1)
+        lane = lax.broadcasted_iota(jnp.int32, (cells, cols), 1)
+        reach = jnp.abs(lag)
+        inside = (lane >= reach) & (lane < cols - reach)
+        image_ref[slot] = jnp.where(inside, filtered, 0.0).reshape(depth, rows, cols)
+        return carry
+
+    lax.fori_loop(0, lags_ref.shape[0], one_lag, 0, unroll=2)
+    for copy in sends:
+        copy.wait_send()
+
+
+def window_shards(bands, roles, *arrays):
+    (vel_index, courant, src_now, src_prev, rec_now, rec_prev) = arrays[:6]
+    (src_pos, src_wavelet, rec_pos, rec_traces, offset_lags) = arrays[6:]
+    depth, rows, cols = vel_index.shape
+    cells = depth * rows
+    full_z, full_y = depth * roles, rows * bands
+    lag_count = offset_lags.shape[0]
+    columns = roles // 2
+    steps = SUB * IMAGES
+    f32, bf16 = jnp.float32, jnp.bfloat16
+    vmem = pl.BlockSpec(memory_space=pltpu.VMEM)
+    smem = pl.BlockSpec(memory_space=pltpu.SMEM)
+    padded = (full_z + 2 * HALO, full_y + 16, cols)
+    image, source, receiver = pl.pallas_call(
+        functools.partial(window_kernel, bands, roles),
+        out_shape=(
+            jax.ShapeDtypeStruct((lag_count, depth, rows, cols), f32),
+            jax.ShapeDtypeStruct((depth, rows, cols), f32),
+            jax.ShapeDtypeStruct((depth, rows, cols), f32),
+        ),
+        in_specs=[vmem, smem, vmem, vmem, vmem, vmem, smem, smem, vmem, vmem, smem],
+        out_specs=(vmem, vmem, vmem),
+        scratch_shapes=[
+            pltpu.VMEM((2, 3 * cells, cols), WIRE),
+            pltpu.VMEM((bands * roles, 3 * cells, cols), WIRE),
+            pltpu.VMEM(padded, f32),
+            pltpu.VMEM(padded, f32),
+            pltpu.VMEM((full_z, full_y, cols), f32),
+            pltpu.VMEM((full_z * full_y, 3 * cols), bf16),
+            pltpu.VMEM((full_z * full_y, cols), f32),
+            pltpu.VMEM((3 * cols, cols), bf16),
+            pltpu.VMEM((steps, cols, cols), bf16),
+            pltpu.VMEM((IMAGES, depth + 2, rows, cols), f32),
+            pltpu.VMEM((IMAGES, 2, depth + 2, rows, cols), f32),
+            pltpu.SemaphoreType.DMA((2 * bands,)),
+            pltpu.SemaphoreType.DMA((2 * bands * columns,)),
+            pltpu.SemaphoreType.DMA((bands * roles,)),
+            pltpu.SemaphoreType.DMA((IMAGES,)),
+            pltpu.SemaphoreType.DMA((IMAGES,)),
+        ],
+        compiler_params=pltpu.CompilerParams(
+            collective_id=0, has_side_effects=True, vmem_limit_bytes=48 * 1024 * 1024
+        ),
+    )(
+        vel_index,
+        courant,
+        src_now,
+        src_prev,
+        rec_now,
+        rec_prev,
+        src_pos,
+        src_wavelet,
+        rec_pos.T,
+        rec_traces.T,
+        offset_lags,
+    )
+    return image.astype(bf16), source, receiver
+
+
+def shards(bands, roles, *arrays):
+    depth, rows, cols = arrays[0].shape
+    sources = arrays[6].shape[0]
+    small = depth * roles * rows * bands * cols <= WINDOW_CELLS
+    fits = roles % 2 == 0 and rows % 8 == 0 and cols % 128 == 0
+    fits = fits and max(rows * bands, sources) <= cols // 2 and arrays[10].shape[0] < cols
+    fits = fits and (depth * rows) % 16 == 0 and arrays[1].shape[0] <= 256
+    if small and fits:
+        return window_shards(bands, roles, *arrays)
+    return tile_shards(*arrays)
+
+
 def solution(mesh):
     placed = (
         P("role", "band", None),
@@ -179,7 +588,7 @@
         P(),
     )
     return jax.shard_map(
-        shards,
+        functools.partial(shards, mesh.shape["band"], mesh.shape["role"]),
         mesh=mesh,
         in_specs=placed,
         out_specs=(

time: 510 us -> 35.6 us (0.07); the launches traced: 502 us -> 34.9 us
  local copies, waits for them, and re-layouts: 172 us -> 7.85 us
  starting transfers between devices: 137 us -> 0 us
  waiting for transfers between devices: 112 us -> 0 us
  other arithmetic: 78.5 us -> 0.74 us
  Pallas kernels: 0 us -> 25.6 us
    ppermute x66 -> x0, starting transfers between devices: 137 us -> none  [the longest x33 94.2 us: padded_2(): lax.ppermute(lax.slice_in_dim(block, block.shape[dim] - width, None, axis...]
    gather x16 -> x0, local copies, waits for them, and re-layouts: 119 us -> none  [the longest x8 60.4 us: product(): lax.dynamic_slice_in_dim(source_pad, max_lag - lag_value, col_cells, 2)]
    ppermute x66 -> x0, waiting for transfers between devices: 112 us -> none  [the longest x33 110 us: padded_2(): lax.ppermute(lax.slice_in_dim(block, 0, width, axis=dim), axis, backward)]
    add x49 -> x0, other arithmetic: 46.6 us -> none  [the longest x32 42.5 us: add_level(): return summed + jnp.where(vel_index == level, courant[level], 0.0)]
    dynamic_slice x48 -> x0, local copies, waits for them, and re-layouts: 43.6 us -> none  [the longest x32 40.6 us: add_level(): return summed + jnp.where(vel_index == level, courant[level], 0.0)]
    pallas_call x0 -> x1, Pallas kernels: none -> 25.6 us  [window_shards(): pl.pallas_call(functools.partial(window_kernel, bands, roles), out_shape=...]
    unnamed x5 -> x0, other arithmetic: 24.9 us -> none
  transfers between devices with their start and end apart: 66 -> 0, of which waited for: 45 -> 0; matrix products, arithmetic and copies ran while one was open for 1% -> 0% of each run, Pallas kernels for 0% -> 0%
where the time goes in v1:
time: 35.6 us; the launch traced here: 34.9 us
  Pallas kernels  25.6 us (72%)
  local copies, waits for them, and re-layouts  7.85 us (22%)
  other arithmetic  0.74 us (2%)
  between operations  0.68 us (2%)
    pallas_call x1, Pallas kernels, window_shards(): pl.pallas_call(functools.partial(window_kernel, bands, roles), out_shape=...  25.6 us
    unnamed x24, local copies, waits for them, and re-layouts  7.85 us
    convert_element_type x1, other arithmetic, window_shards(): return (image.astype(bf16), source, receiver)  0.74 us

profile of v1, /device:TPU:0, one launch (start us, length us, event | category | flops | bytes accessed | tf_op | source)
XLA Modules:
  0.0 34.9 jit_solution(14535718632896456812)
XLA Ops:
  0.6 0.0 copy-start.7
  0.6 0.0 copy-start.9
  0.7 0.0 copy-start.10
  0.7 0.7 %copy-done.7 = s32[4,3]{1,0:T(4,128)S(1)} copy-done((s32[4,3]{1,0:T(4,128)S(1)}, s32[4,3]{1,0:T(4,128)}, u32[]{:S(2)}) %copy-start.7) | copy-done | bytes 72
  1.3 0.0 copy-done.9
  1.3 0.0 copy-done.10
  1.3 0.0 copy-start
  1.3 0.9 %copy-done = f32[4096,16]{0,1:T(8,128)S(1)} copy-done((f32[4096,16]{0,1:T(8,128)S(1)}, f32[4096,16]{0,1:T(8,128)}, u32[]{:S(2)}) %copy-start) | copy-done | bytes 262168
  2.3 0.8 %copy-done.1 = s32[4096,2]{0,1:T(2,128)S(1)} copy-done((s32[4096,2]{0,1:T(2,128)S(1)}, s32[4096,2]{0,1:T(2,128)}, u32[]{:S(2)}) %copy-start.1) | copy-done | bytes 32792
  3.0 0.0 copy-start.2
  3.0 0.7 %copy-done.2 = s32[4,8,128]{2,1,0:T(8,128)S(1)} copy-done((s32[4,8,128]{2,1,0:T(8,128)S(1)}, s32[4,8,128]{2,1,0:T(8,128)}, u32[]{:S(2)}) %copy-start.2) | copy-done | bytes 16408
  3.8 0.0 copy-start.3
  3.8 0.7 %copy-done.3 = f32[4,8,128]{2,1,0:T(8,128)S(1)} copy-done((f32[4,8,128]{2,1,0:T(8,128)S(1)}, f32[4,8,128]{2,1,0:T(8,128)}, u32[]{:S(2)}) %copy-start.3) | copy-done | bytes 16408
  4.5 0.0 copy-start.4
  4.5 0.7 %copy-done.4 = f32[4,8,128]{2,1,0:T(8,128)S(1)} copy-done((f32[4,8,128]{2,1,0:T(8,128)S(1)}, f32[4,8,128]{2,1,0:T(8,128)}, u32[]{:S(2)}) %copy-start.4) | copy-done | bytes 16408
  5.2 0.0 copy-start.5
  5.2 0.7 %copy-done.5 = f32[4,8,128]{2,1,0:T(8,128)S(1)} copy-done((f32[4,8,128]{2,1,0:T(8,128)S(1)}, f32[4,8,128]{2,1,0:T(8,128)}, u32[]{:S(2)}) %copy-start.5) | copy-done | bytes 16408
  5.9 0.7 %copy-done.6 = f32[4,8,128]{2,1,0:T(8,128)S(1)} copy-done((f32[4,8,128]{2,1,0:T(8,128)S(1)}, f32[4,8,128]{2,1,0:T(8,128)}, u32[]{:S(2)}) %copy-start.6) | copy-done | bytes 16408
  6.6 0.0 copy-start.8
  6.6 0.7 %copy-done.8 = f32[4,16]{1,0:T(4,128)S(1)} copy-done((f32[4,16]{1,0:T(4,128)S(1)}, f32[4,16]{1,0:T(4,128)}, u32[]{:S(2)}) %copy-start.8) | copy-done | bytes 280
  7.3 25.6 %shard_map.130 = (f32[32,4,8,128]{3,2,1,0:T(8,128)S(1)}, f32[4,8,128]{2,1,0:T(8,128)S(1)}, f32[4,8,128]{2,1,0:T(8,128)S(1)}) custom-call(s32[4,8,128]{2,1,0:T(8,128)S(1)} %copy-done.2, f32[32]{0:T(128)S(1)} %copy-done.9, f32[4,8,128]{2,1,0:T(8,128)S(1)} %copy-done.3, f32[4,8,128]{2,1,0:T(8,128)S(1)} %copy-done.4, f32[4,8,128]{2,1,0:T(8,128)S(1)} %copy-done.5, ...), custom_call_target="tpu_custom_call" | custom-call | tf_op jit(solution)/shard_map/pallas_call | solution.py:518
  32.9 0.7 %convert_element_type.3 = bf16[32,4,8,128]{3,2,1,0:T(8,128)(2,1)} convert(f32[32,4,8,128]{3,2,1,0:T(8,128)S(1)} %get-tuple-element.6) | non-fusion elementwise | flops 131072 | bytes 786432 | tf_op jit(solution)/shard_map/convert_element_type | solution.py:561
  33.7 0.6 %copy.16 = f32[4,8,128]{2,1,0:T(8,128)} copy(f32[4,8,128]{2,1,0:T(8,128)S(1)} %get-tuple-element.13) | data formatting | bytes 32768
  34.3 0.6 %copy.17 = f32[4,8,128]{2,1,0:T(8,128)} copy(f32[4,8,128]{2,1,0:T(8,128)S(1)} %get-tuple-element.14) | data formatting | bytes 32768
  (2 shorter events, 0.0 us)
Async XLA Ops:
  0.6 0.7 %copy-start.7 = (s32[4,3]{1,0:T(4,128)S(1)}, s32[4,3]{1,0:T(4,128)}, u32[]{:S(2)}) copy-start(s32[4,3]{1,0:T(4,128)} %src_pos_ref.1) | copy-start | bytes 148
  0.6 0.7 %copy-start.9 = (f32[32]{0:T(128)S(1)}, f32[32]{0:T(128)}, u32[]{:S(2)}) copy-start(f32[32]{0:T(128)} %courant_ref.1) | copy-start | bytes 388
  0.7 0.7 %copy-start.10 = (s32[32]{0:T(128)S(1)}, s32[32]{0:T(128)}, u32[]{:S(2)}) copy-start(s32[32]{0:T(128)} %lags_ref.1) | copy-start | bytes 388
  1.3 1.0 %copy-start = (f32[4096,16]{0,1:T(8,128)S(1)}, f32[4096,16]{0,1:T(8,128)}, u32[]{:S(2)}) copy-start(f32[4096,16]{0,1:T(8,128)} %param.20) | copy-start | bytes 786436
  2.3 0.8 %copy-start.1 = (s32[4096,2]{0,1:T(2,128)S(1)}, s32[4096,2]{0,1:T(2,128)}, u32[]{:S(2)}) copy-start(s32[4096,2]{0,1:T(2,128)} %param.19) | copy-start | bytes 98308
  3.0 0.7 %copy-start.2 = (s32[4,8,128]{2,1,0:T(8,128)S(1)}, s32[4,8,128]{2,1,0:T(8,128)}, u32[]{:S(2)}) copy-start(s32[4,8,128]{2,1,0:T(8,128)} %vel_ref.1) | copy-start | bytes 49156
  3.8 0.7 %copy-start.3 = (f32[4,8,128]{2,1,0:T(8,128)S(1)}, f32[4,8,128]{2,1,0:T(8,128)}, u32[]{:S(2)}) copy-start(f32[4,8,128]{2,1,0:T(8,128)} %src_now_ref.1) | copy-start | bytes 49156
  4.5 0.7 %copy-start.4 = (f32[4,8,128]{2,1,0:T(8,128)S(1)}, f32[4,8,128]{2,1,0:T(8,128)}, u32[]{:S(2)}) copy-start(f32[4,8,128]{2,1,0:T(8,128)} %src_prev_ref.1) | copy-start | bytes 49156
  5.2 0.7 %copy-start.5 = (f32[4,8,128]{2,1,0:T(8,128)S(1)}, f32[4,8,128]{2,1,0:T(8,128)}, u32[]{:S(2)}) copy-start(f32[4,8,128]{2,1,0:T(8,128)} %rec_now_ref.1) | copy-start | bytes 49156
  5.9 0.7 %copy-start.6 = (f32[4,8,128]{2,1,0:T(8,128)S(1)}, f32[4,8,128]{2,1,0:T(8,128)}, u32[]{:S(2)}) copy-start(f32[4,8,128]{2,1,0:T(8,128)} %rec_prev_ref.1) | copy-start | bytes 49156
  6.6 0.7 %copy-start.8 = (f32[4,16]{1,0:T(4,128)S(1)}, f32[4,16]{1,0:T(4,128)}, u32[]{:S(2)}) copy-start(f32[4,16]{1,0:T(4,128)} %src_wave_ref.1) | copy-start | bytes 772

commit v2 on v1

--- a/solution.py
+++ b/solution.py
@@ -191,37 +191,52 @@
 def window_kernel(
     bands,
     roles,
-    vel_ref,
-    courant_ref,
-    src_now_ref,
-    src_prev_ref,
-    rec_now_ref,
-    rec_prev_ref,
-    src_pos_ref,
-    src_wave_ref,
-    rec_pos_ref,
-    rec_trace_ref,
-    lags_ref,
-    image_ref,
-    src_out_ref,
-    rec_out_ref,
-    out_buf,
-    blocks,
-    field_a,
-    field_b,
-    speed_ref,
-    split_ref,
-    inline_ref,
-    base_ref,
-    inject_ref,
-    stage_ref,
-    snap_ref,
-    near_send,
-    far_send,
-    block_recv,
-    snap_send,
-    snap_recv,
+    *refs,
 ):
+    inputs, outputs, held = refs[:11], refs[11:14], refs[14:25]
+    (
+        vel_ref,
+        courant_ref,
+        src_now_ref,
+        src_prev_ref,
+        rec_now_ref,
+        rec_prev_ref,
+        src_pos_ref,
+        src_wave_ref,
+        rec_pos_ref,
+        rec_trace_ref,
+        lags_ref,
+    ) = held
+    image_ref, src_out_ref, rec_out_ref = outputs
+    (
+        out_buf,
+        blocks,
+        field_a,
+        field_b,
+        speed_ref,
+        split_ref,
+        inline_ref,
+        base_ref,
+        inject_ref,
+        stage_ref,
+        snap_ref,
+        near_send,
+        far_send,
+        block_recv,
+        snap_send,
+        snap_recv,
+        lend_ref,
+        in_sem,
+        lend_send,
+        lend_recv,
+    ) = refs[25:]
+    fetches = [
+        pltpu.make_async_copy(given, kept, in_sem.at[at])
+        for at, (given, kept) in enumerate(zip(inputs, held))
+    ]
+    for fetch in fetches:
+        fetch.start()
+    inject_ref[...] = jnp.zeros_like(inject_ref)
     depth, rows, cols = vel_ref.shape
     full_z, full_y = depth * roles, rows * bands
     cells = depth * rows
@@ -261,6 +276,8 @@
         )
         greeted += 1
 
+    for at in (0, 2, 3, 4, 5):
+        fetches[at].wait()
     index = vel_ref[...].astype(f32).reshape(cells, cols)
     for side, now_ref, prev_ref in ((0, src_now_ref, src_prev_ref), (1, rec_now_ref, rec_prev_ref)):
         now = now_ref[...].reshape(cells, cols)
@@ -312,7 +329,8 @@
     for step in range(1, columns):
         pass_on(step, out_buf.at[core], own, step)
 
-    inject_ref[...] = jnp.zeros_like(inject_ref)
+    for at in (1, 6, 7, 8, 9, 10):
+        fetches[at].wait()
     lines = split_ref.shape[0]
     half = cols // 2
     row_at = lax.broadcasted_iota(jnp.int32, (lines, cols), 0)
@@ -342,26 +360,37 @@
             inject_ref[tick, 0:height] = high
             inject_ref[tick, half : half + height] = low
 
+    high, low = split_two(inline_matrix(cols))
+    base_ref[0:cols] = high
+    base_ref[cols : 2 * cols] = high
+    base_ref[2 * cols : 3 * cols] = low
+    field_a[...] = jnp.zeros_like(field_a)
+    field_b[...] = jnp.zeros_like(field_b)
+
     @pl.when(core == 1)
     def _():
         split_ref[:, 2 * cols : 3 * cols] = jnp.where(
             (row_at < full_y) & (row_at == lane_low), 1.0, 0.0
         ).astype(jnp.bfloat16)
-        count = rec_pos_ref.shape[1]
-        chunk = min(512, count)
-        total = jnp.zeros((2 * steps * full_y, cols), f32)
-        for at in range(0, count, chunk):
-            size = min(chunk, count - at)
+
+    share = steps // 2
+    first = pl.multiple_of(share * (1 - core), share)
+    count = rec_pos_ref.shape[1]
+    chunk = min(512, count)
+
+    def add_receivers(total, start, stop):
+        for at in range(start, stop, chunk):
+            size = min(chunk, stop - at)
             y_at = rec_pos_ref[0:1, at : at + size]
             x_at = rec_pos_ref[1:2, at : at + size]
             in_row = lax.broadcasted_iota(jnp.int32, (full_y, size), 0) == y_at
             in_col = lax.broadcasted_iota(jnp.int32, (cols, size), 0) == x_at
             in_col = jnp.where(in_col, 1.0, 0.0).astype(jnp.bfloat16)
-            amounts = rec_trace_ref[:, at : at + size]
+            amounts = rec_trace_ref[pl.ds(first, share), at : at + size]
             high = amounts.astype(jnp.bfloat16).astype(f32)
             parts = []
             for part in (high, amounts - high):
-                for tick in range(steps):
+                for tick in range(share):
                     parts.append(jnp.where(in_row, part[tick : tick + 1], 0.0).astype(jnp.bfloat16))
             total = total + lax.dot_general(
                 jnp.concatenate(parts, axis=0),
@@ -369,18 +398,10 @@
                 (((1,), (1,)), ((), ())),
                 preferred_element_type=f32,
             )
-        size = steps * full_y
-        high, low = split_two(total[0:size] + total[size : 2 * size])
-        for tick in range(steps):
-            inject_ref[tick, 0:full_y] = high[tick * full_y : (tick + 1) * full_y]
-            inject_ref[tick, half : half + full_y] = low[tick * full_y : (tick + 1) * full_y]
-
-    high, low = split_two(inline_matrix(cols))
-    base_ref[0:cols] = high
-    base_ref[cols : 2 * cols] = high
-    base_ref[2 * cols : 3 * cols] = low
-    field_a[...] = jnp.zeros_like(field_a)
-    field_b[...] = jnp.zeros_like(field_b)
+        return total
+
+    middle = count // 2 // chunk * chunk
+    added = add_receivers(jnp.zeros((2 * share * full_y, cols), f32), 0, middle)
 
     slot = band * roles + 2 * column + 1 - core
     landed(slot)
@@ -392,12 +413,31 @@
             landed(slot)
             for step in range(1, columns):
                 pass_on(step, blocks.at[slot], slot, (2 * hop + side) * columns + step)
-    for step in range(1, columns):
-        other = lax.rem(column + step, columns)
-        for at_band in range(bands):
-            for side in range(2):
-                landed(at_band * roles + 2 * other + side)
-    blocks[own] = out_buf[core]
+    added = add_receivers(added, middle, count)
+    size = share * full_y
+    high, low = split_two(added[0:size] + added[size : 2 * size])
+    lend_ref[0] = high.reshape(share, full_y, cols)
+    lend_ref[1] = low.reshape(share, full_y, cols)
+
+    def lend_copy(part):
+        return pltpu.make_async_remote_copy(
+            src_ref=lend_ref.at[part],
+            dst_ref=inject_ref.at[pl.ds(share, share), pl.ds(part * half, full_y)],
+            send_sem=lend_send.at[part],
+            recv_sem=lend_recv.at[part],
+            device_id=partner,
+            device_id_type=MESH,
+        )
+
+    @pl.when(core == 0)
+    def _():
+        for part in range(2):
+            lend_copy(part).start()
+
+    @pl.when(core == 1)
+    def _():
+        for part in range(2):
+            inject_ref[0:share, part * half : part * half + full_y] = lend_ref[part]
 
     def table(values):
         found = jnp.zeros(values.shape, f32)
@@ -405,18 +445,31 @@
             found = jnp.where(values == float(level), courant_ref[level], found)
         return found
 
-    for at_role in range(roles):
-        for at_band in range(bands):
-            block = blocks[at_band * roles + at_role].astype(f32)
-            now = block[0:cells].reshape(depth, rows, cols)
-            prev = now - block[cells : 2 * cells].reshape(depth, rows, cols)
-            z_part = pl.ds(HALO + depth * at_role, depth)
-            y_part = pl.ds(y0 + rows * at_band, rows)
-            field_a[z_part, y_part, :] = now
-            field_b[z_part, y_part, :] = prev
-            speed_ref[pl.ds(depth * at_role, depth), pl.ds(rows * at_band, rows), :] = table(
-                block[2 * cells : 3 * cells]
-            ).reshape(depth, rows, cols)
+    def unpack(at_band, at_role, block):
+        now = block[0:cells].reshape(depth, rows, cols)
+        prev = now - block[cells : 2 * cells].reshape(depth, rows, cols)
+        z_part = pl.ds(HALO + depth * at_role, depth)
+        y_part = pl.ds(pl.multiple_of(y0 + rows * at_band, rows), rows)
+        field_a[z_part, y_part, :] = now
+        field_b[z_part, y_part, :] = prev
+        speed_ref[pl.ds(depth * at_role, depth), pl.ds(pl.multiple_of(rows * at_band, rows), rows), :] = table(
+            block[2 * cells : 3 * cells]
+        ).reshape(depth, rows, cols)
+
+    for hop in range(bands):
+        for side in range(2):
+            at_band, at_role = lax.rem(band + hop, bands), 2 * column + lax.rem(core + side, 2)
+            if hop == 0 and side == 0:
+                unpack(band, role, out_buf[core].astype(f32))
+            else:
+                unpack(at_band, at_role, blocks[at_band * roles + at_role].astype(f32))
+    for hop in range(bands):
+        for step in range(1, columns):
+            for side in range(2):
+                at_band = lax.rem(band + hop, bands)
+                at_role = 2 * lax.rem(column + step, columns) + lax.rem(core + side, 2)
+                landed(at_band * roles + at_role)
+                unpack(at_band, at_role, blocks[at_band * roles + at_role].astype(f32))
 
     own_z = pl.ds(HALO + depth * role, depth)
     own_y = pl.ds(pl.multiple_of(y0 + rows * band, rows), rows)
@@ -465,6 +518,11 @@
         )
 
     def one_image(snapshot, carry):
+        @pl.when((snapshot == IMAGES // 2) & (core == 1))
+        def _():
+            for part in range(2):
+                lend_copy(part).wait_recv()
+
         for pair in range(SUB // 2):
             advance(SUB * snapshot + 2 * pair, field_a, field_b)
             advance(SUB * snapshot + 2 * pair + 1, field_b, field_a)
@@ -497,15 +555,19 @@
         image_ref[slot] = jnp.where(inside, filtered, 0.0).reshape(depth, rows, cols)
         return carry
 
-    lax.fori_loop(0, lags_ref.shape[0], one_lag, 0, unroll=2)
+    lax.fori_loop(0, lags_ref.shape[0], one_lag, 0, unroll=8)
+    @pl.when(core == 0)
+    def _():
+        for part in range(2):
+            lend_copy(part).wait_send()
+
     for copy in sends:
         copy.wait_send()
 
 
 def window_shards(bands, roles, *arrays):
-    (vel_index, courant, src_now, src_prev, rec_now, rec_prev) = arrays[:6]
-    (src_pos, src_wavelet, rec_pos, rec_traces, offset_lags) = arrays[6:]
-    depth, rows, cols = vel_index.shape
+    rec_pos, rec_traces, offset_lags = arrays[8:]
+    depth, rows, cols = arrays[0].shape
     cells = depth * rows
     full_z, full_y = depth * roles, rows * bands
     lag_count = offset_lags.shape[0]
@@ -513,7 +575,9 @@
     steps = SUB * IMAGES
     f32, bf16 = jnp.float32, jnp.bfloat16
     vmem = pl.BlockSpec(memory_space=pltpu.VMEM)
-    smem = pl.BlockSpec(memory_space=pltpu.SMEM)
+    hbm = pl.BlockSpec(memory_space=pltpu.HBM)
+    arrays = arrays[:8] + (rec_pos.T, rec_traces.T, offset_lags)
+    places = [pltpu.SMEM if at in (1, 6, 7, 10) else pltpu.VMEM for at in range(len(arrays))]
     padded = (full_z + 2 * HALO, full_y + 16, cols)
     image, source, receiver = pl.pallas_call(
         functools.partial(window_kernel, bands, roles),
@@ -522,9 +586,10 @@
             jax.ShapeDtypeStruct((depth, rows, cols), f32),
             jax.ShapeDtypeStruct((depth, rows, cols), f32),
         ),
-        in_specs=[vmem, smem, vmem, vmem, vmem, vmem, smem, smem, vmem, vmem, smem],
+        in_specs=[hbm] * len(arrays),
         out_specs=(vmem, vmem, vmem),
-        scratch_shapes=[
+        scratch_shapes=[place(array.shape, array.dtype) for place, array in zip(places, arrays)]
+        + [
             pltpu.VMEM((2, 3 * cells, cols), WIRE),
             pltpu.VMEM((bands * roles, 3 * cells, cols), WIRE),
             pltpu.VMEM(padded, f32),
@@ -541,23 +606,15 @@
             pltpu.SemaphoreType.DMA((bands * roles,)),
             pltpu.SemaphoreType.DMA((IMAGES,)),
             pltpu.SemaphoreType.DMA((IMAGES,)),
+            pltpu.VMEM((2, steps // 2, full_y, cols), bf16),
+            pltpu.SemaphoreType.DMA((len(arrays),)),
+            pltpu.SemaphoreType.DMA((2,)),
+            pltpu.SemaphoreType.DMA((2,)),
         ],
         compiler_params=pltpu.CompilerParams(
             collective_id=0, has_side_effects=True, vmem_limit_bytes=48 * 1024 * 1024
         ),
-    )(
-        vel_index,
-        courant,
-        src_now,
-        src_prev,
-        rec_now,
-        rec_prev,
-        src_pos,
-        src_wavelet,
-        rec_pos.T,
-        rec_traces.T,
-        offset_lags,
-    )
+    )(*arrays)
     return image.astype(bf16), source, receiver
 
 

time: 35.6 us -> 33.8 us (0.949)
  Pallas kernels: 25.6 us -> 23.9 us
    pallas_call x1, Pallas kernels: 25.6 us -> 23.9 us  [window_shards(): pl.pallas_call(functools.partial(window_kernel, bands, roles), out_shape=...]
where the time goes in v2:
time: 33.8 us; the launch traced here: 33.2 us
  Pallas kernels  23.9 us (71%)
  local copies, waits for them, and re-layouts  7.85 us (23%)
  other arithmetic  0.74 us (2%)
  between operations  0.68 us (2%)
    pallas_call x1, Pallas kernels, window_shards(): pl.pallas_call(functools.partial(window_kernel, bands, roles), out_shape=...  23.9 us
    unnamed x24, local copies, waits for them, and re-layouts  7.85 us
    convert_element_type x1, other arithmetic, window_shards(): return (image.astype(bf16), source, receiver)  0.74 us

profile of v2, /device:TPU:0, one launch (start us, length us, event | category | flops | bytes accessed | tf_op | source)
XLA Modules:
  0.0 33.2 jit_solution(8711454576713860672)
XLA Ops:
  0.6 0.0 copy-start.7
  0.6 0.0 copy-start.9
  0.7 0.0 copy-start.10
  0.7 0.7 %copy-done.7 = s32[4,3]{1,0:T(4,128)S(1)} copy-done((s32[4,3]{1,0:T(4,128)S(1)}, s32[4,3]{1,0:T(4,128)}, u32[]{:S(2)}) %copy-start.7) | copy-done | bytes 72
  1.3 0.0 copy-done.9
  1.3 0.0 copy-done.10
  1.3 0.0 copy-start
  1.3 0.9 %copy-done = f32[4096,16]{0,1:T(8,128)S(1)} copy-done((f32[4096,16]{0,1:T(8,128)S(1)}, f32[4096,16]{0,1:T(8,128)}, u32[]{:S(2)}) %copy-start) | copy-done | bytes 262168
  2.3 0.0 copy-start.1
  2.3 0.8 %copy-done.1 = s32[4096,2]{0,1:T(2,128)S(1)} copy-done((s32[4096,2]{0,1:T(2,128)S(1)}, s32[4096,2]{0,1:T(2,128)}, u32[]{:S(2)}) %copy-start.1) | copy-done | bytes 32792
  3.0 0.0 copy-start.2
  3.0 0.7 %copy-done.2 = s32[4,8,128]{2,1,0:T(8,128)S(1)} copy-done((s32[4,8,128]{2,1,0:T(8,128)S(1)}, s32[4,8,128]{2,1,0:T(8,128)}, u32[]{:S(2)}) %copy-start.2) | copy-done | bytes 16408
  3.8 0.0 copy-start.3
  3.8 0.7 %copy-done.3 = f32[4,8,128]{2,1,0:T(8,128)S(1)} copy-done((f32[4,8,128]{2,1,0:T(8,128)S(1)}, f32[4,8,128]{2,1,0:T(8,128)}, u32[]{:S(2)}) %copy-start.3) | copy-done | bytes 16408
  4.5 0.0 copy-start.4
  4.5 0.7 %copy-done.4 = f32[4,8,128]{2,1,0:T(8,128)S(1)} copy-done((f32[4,8,128]{2,1,0:T(8,128)S(1)}, f32[4,8,128]{2,1,0:T(8,128)}, u32[]{:S(2)}) %copy-start.4) | copy-done | bytes 16408
  5.2 0.0 copy-start.5
  5.2 0.7 %copy-done.5 = f32[4,8,128]{2,1,0:T(8,128)S(1)} copy-done((f32[4,8,128]{2,1,0:T(8,128)S(1)}, f32[4,8,128]{2,1,0:T(8,128)}, u32[]{:S(2)}) %copy-start.5) | copy-done | bytes 16408
  5.9 0.7 %copy-done.6 = f32[4,8,128]{2,1,0:T(8,128)S(1)} copy-done((f32[4,8,128]{2,1,0:T(8,128)S(1)}, f32[4,8,128]{2,1,0:T(8,128)}, u32[]{:S(2)}) %copy-start.6) | copy-done | bytes 16408
  6.6 0.7 %copy-done.8 = f32[4,16]{1,0:T(4,128)S(1)} copy-done((f32[4,16]{1,0:T(4,128)S(1)}, f32[4,16]{1,0:T(4,128)}, u32[]{:S(2)}) %copy-start.8) | copy-done | bytes 280
  7.3 23.9 %shard_map.130 = (f32[32,4,8,128]{3,2,1,0:T(8,128)S(1)}, f32[4,8,128]{2,1,0:T(8,128)S(1)}, f32[4,8,128]{2,1,0:T(8,128)S(1)}) custom-call(s32[4,8,128]{2,1,0:T(8,128)S(1)} %copy-done.2, f32[32]{0:T(128)S(1)} %copy-done.9, f32[4,8,128]{2,1,0:T(8,128)S(1)} %copy-done.3, f32[4,8,128]{2,1,0:T(8,128)S(1)} %copy-done.4, f32[4,8,128]{2,1,0:T(8,128)S(1)} %copy-done.5, ...), custom_call_target="tpu_custom_call" | custom-call | tf_op jit(solution)/shard_map/pallas_call | solution.py:582
  31.2 0.7 %convert_element_type.3 = bf16[32,4,8,128]{3,2,1,0:T(8,128)(2,1)} convert(f32[32,4,8,128]{3,2,1,0:T(8,128)S(1)} %get-tuple-element.6) | non-fusion elementwise | flops 131072 | bytes 786432 | tf_op jit(solution)/shard_map/convert_element_type | solution.py:618
  32.0 0.6 %copy.16 = f32[4,8,128]{2,1,0:T(8,128)} copy(f32[4,8,128]{2,1,0:T(8,128)S(1)} %get-tuple-element.13) | data formatting | bytes 32768
  32.6 0.6 %copy.17 = f32[4,8,128]{2,1,0:T(8,128)} copy(f32[4,8,128]{2,1,0:T(8,128)S(1)} %get-tuple-element.14) | data formatting | bytes 32768
  (2 shorter events, 0.0 us)
Async XLA Ops:
  0.6 0.7 %copy-start.7 = (s32[4,3]{1,0:T(4,128)S(1)}, s32[4,3]{1,0:T(4,128)}, u32[]{:S(2)}) copy-start(s32[4,3]{1,0:T(4,128)} %refs_6_.1) | copy-start | bytes 148
  0.6 0.7 %copy-start.9 = (f32[32]{0:T(128)S(1)}, f32[32]{0:T(128)}, u32[]{:S(2)}) copy-start(f32[32]{0:T(128)} %refs_1_.1) | copy-start | bytes 388
  0.7 0.7 %copy-start.10 = (s32[32]{0:T(128)S(1)}, s32[32]{0:T(128)}, u32[]{:S(2)}) copy-start(s32[32]{0:T(128)} %refs_10_.1) | copy-start | bytes 388
  1.3 1.0 %copy-start = (f32[4096,16]{0,1:T(8,128)S(1)}, f32[4096,16]{0,1:T(8,128)}, u32[]{:S(2)}) copy-start(f32[4096,16]{0,1:T(8,128)} %param.20) | copy-start | bytes 786436
  2.3 0.8 %copy-start.1 = (s32[4096,2]{0,1:T(2,128)S(1)}, s32[4096,2]{0,1:T(2,128)}, u32[]{:S(2)}) copy-start(s32[4096,2]{0,1:T(2,128)} %param.19) | copy-start | bytes 98308
  3.0 0.7 %copy-start.2 = (s32[4,8,128]{2,1,0:T(8,128)S(1)}, s32[4,8,128]{2,1,0:T(8,128)}, u32[]{:S(2)}) copy-start(s32[4,8,128]{2,1,0:T(8,128)} %refs_0_.1) | copy-start | bytes 49156
  3.8 0.7 %copy-start.3 = (f32[4,8,128]{2,1,0:T(8,128)S(1)}, f32[4,8,128]{2,1,0:T(8,128)}, u32[]{:S(2)}) copy-start(f32[4,8,128]{2,1,0:T(8,128)} %refs_2_.1) | copy-start | bytes 49156
  4.5 0.7 %copy-start.4 = (f32[4,8,128]{2,1,0:T(8,128)S(1)}, f32[4,8,128]{2,1,0:T(8,128)}, u32[]{:S(2)}) copy-start(f32[4,8,128]{2,1,0:T(8,128)} %refs_3_.1) | copy-start | bytes 49156
  5.2 0.7 %copy-start.5 = (f32[4,8,128]{2,1,0:T(8,128)S(1)}, f32[4,8,128]{2,1,0:T(8,128)}, u32[]{:S(2)}) copy-start(f32[4,8,128]{2,1,0:T(8,128)} %refs_4_.1) | copy-start | bytes 49156
  5.9 0.7 %copy-start.6 = (f32[4,8,128]{2,1,0:T(8,128)S(1)}, f32[4,8,128]{2,1,0:T(8,128)}, u32[]{:S(2)}) copy-start(f32[4,8,128]{2,1,0:T(8,128)} %refs_5_.1) | copy-start | bytes 49156
  6.6 0.7 %copy-start.8 = (f32[4,16]{1,0:T(4,128)S(1)}, f32[4,16]{1,0:T(4,128)}, u32[]{:S(2)}) copy-start(f32[4,16]{1,0:T(4,128)} %refs_7_.1) | copy-start | bytes 772

commit v3 on v2

--- a/solution.py
+++ b/solution.py
@@ -13,6 +13,7 @@
 WINDOW_CELLS = 1 << 17
 MESH = pl.DeviceIdType.MESH
 WIRE = jnp.bfloat16
+VMEM_GRANT = 64 * 1024 * 1024
 
 
 STENCIL_WEIGHTS = (-205.0 / 72.0, 8.0 / 5.0, -1.0 / 5.0, 8.0 / 315.0, -1.0 / 560.0)
@@ -226,6 +227,8 @@
         snap_send,
         snap_recv,
         lend_ref,
+        image_buf,
+        out_sem,
         in_sem,
         lend_send,
         lend_recv,
@@ -534,8 +537,12 @@
     lax.fori_loop(0, IMAGES, one_image, 0)
     for snapshot in range(IMAGES):
         snap_copy(snapshot).wait()
-    src_out_ref[...] = snap_ref[IMAGES - 1, 0, 1 : 1 + depth]
-    rec_out_ref[...] = snap_ref[IMAGES - 1, 1, 1 : 1 + depth]
+    results = [
+        pltpu.make_async_copy(snap_ref.at[IMAGES - 1, side, pl.ds(1, depth)], kept, out_sem.at[side])
+        for side, kept in enumerate((src_out_ref, rec_out_ref))
+    ]
+    for result in results:
+        result.start()
 
     def one_lag(slot, carry):
         lag = lags_ref[slot]
@@ -552,10 +559,21 @@
         lane = lax.broadcasted_iota(jnp.int32, (cells, cols), 1)
         reach = jnp.abs(lag)
         inside = (lane >= reach) & (lane < cols - reach)
-        image_ref[slot] = jnp.where(inside, filtered, 0.0).reshape(depth, rows, cols)
+        at = pl.multiple_of(slot * cells, cells)
+        image_buf[pl.ds(at, cells)] = jnp.where(inside, filtered, 0.0).astype(jnp.bfloat16)
         return carry
 
-    lax.fori_loop(0, lags_ref.shape[0], one_lag, 0, unroll=8)
+    lag_count = lags_ref.shape[0]
+    group = -(-lag_count // 4)
+    for turn, start in enumerate(range(0, lag_count, group)):
+        stop = min(start + group, lag_count)
+        lax.fori_loop(start, stop, one_lag, 0, unroll=group)
+        part = pl.ds(start * cells, (stop - start) * cells)
+        result = pltpu.make_async_copy(image_buf.at[part], image_ref.at[part], out_sem.at[2 + turn])
+        result.start()
+        results.append(result)
+    for result in results:
+        result.wait()
     @pl.when(core == 0)
     def _():
         for part in range(2):
@@ -563,6 +581,14 @@
 
     for copy in sends:
         copy.wait_send()
+
+
+def hand_over(*refs):
+    copies = [pltpu.make_async_copy(refs[at], refs[3 + at], refs[6].at[at]) for at in range(3)]
+    for copy in copies:
+        copy.start()
+    for copy in copies:
+        copy.wait()
 
 
 def window_shards(bands, roles, *arrays):
@@ -574,20 +600,19 @@
     columns = roles // 2
     steps = SUB * IMAGES
     f32, bf16 = jnp.float32, jnp.bfloat16
-    vmem = pl.BlockSpec(memory_space=pltpu.VMEM)
     hbm = pl.BlockSpec(memory_space=pltpu.HBM)
     arrays = arrays[:8] + (rec_pos.T, rec_traces.T, offset_lags)
     places = [pltpu.SMEM if at in (1, 6, 7, 10) else pltpu.VMEM for at in range(len(arrays))]
     padded = (full_z + 2 * HALO, full_y + 16, cols)
-    image, source, receiver = pl.pallas_call(
+    results = pl.pallas_call(
         functools.partial(window_kernel, bands, roles),
         out_shape=(
-            jax.ShapeDtypeStruct((lag_count, depth, rows, cols), f32),
+            jax.ShapeDtypeStruct((lag_count * cells, cols), bf16),
             jax.ShapeDtypeStruct((depth, rows, cols), f32),
             jax.ShapeDtypeStruct((depth, rows, cols), f32),
         ),
         in_specs=[hbm] * len(arrays),
-        out_specs=(vmem, vmem, vmem),
+        out_specs=(hbm, hbm, hbm),
         scratch_shapes=[place(array.shape, array.dtype) for place, array in zip(places, arrays)]
         + [
             pltpu.VMEM((2, 3 * cells, cols), WIRE),
@@ -607,15 +632,25 @@
             pltpu.SemaphoreType.DMA((IMAGES,)),
             pltpu.SemaphoreType.DMA((IMAGES,)),
             pltpu.VMEM((2, steps // 2, full_y, cols), bf16),
+            pltpu.VMEM((lag_count * cells, cols), bf16),
+            pltpu.SemaphoreType.DMA((6,)),
             pltpu.SemaphoreType.DMA((len(arrays),)),
             pltpu.SemaphoreType.DMA((2,)),
             pltpu.SemaphoreType.DMA((2,)),
         ],
         compiler_params=pltpu.CompilerParams(
-            collective_id=0, has_side_effects=True, vmem_limit_bytes=48 * 1024 * 1024
+            collective_id=0, has_side_effects=True, vmem_limit_bytes=VMEM_GRANT
         ),
     )(*arrays)
-    return image.astype(bf16), source, receiver
+    image, source, receiver = pl.pallas_call(
+        hand_over,
+        out_shape=tuple(jax.ShapeDtypeStruct(result.shape, result.dtype) for result in results),
+        in_specs=[hbm] * 3,
+        out_specs=(hbm, hbm, hbm),
+        scratch_shapes=[pltpu.SemaphoreType.DMA((3,))],
+        compiler_params=pltpu.CompilerParams(vmem_limit_bytes=VMEM_GRANT),
+    )(*results)
+    return image.reshape(lag_count, depth, rows, cols), source, receiver
 
 
 def shards(bands, roles, *arrays):

time: 33.8 us -> 36.4 us (1.077)
  Pallas kernels: 23.9 us -> 35.5 us
  local copies, waits for them, and re-layouts: 7.85 us -> 0 us
  other arithmetic: 0.74 us -> 0 us
    pallas_call x0 -> x1, Pallas kernels: none -> 10.1 us  [window_shards(): pl.pallas_call(hand_over, out_shape=tuple((jax.ShapeDtypeStruct(result.sh...]
    unnamed x24 -> x0, local copies, waits for them, and re-layouts: 7.85 us -> none
    pallas_call x1, Pallas kernels: 23.9 us -> 25.4 us  [window_shards(): pl.pallas_call(functools.partial(window_kernel, bands, roles), out_shape=...]
    convert_element_type x1 -> x0, other arithmetic: 0.74 us -> none  [window_shards(): return (image.astype(bf16), source, receiver)]
where the time goes in v3:
time: 36.4 us; the launch traced here: 36.1 us
  Pallas kernels  35.5 us (98%)
  between operations  0.64 us (2%)
    pallas_call x1, Pallas kernels, window_shards(): pl.pallas_call(functools.partial(window_kernel, bands, roles), out_shape=...  25.4 us
    pallas_call x1, Pallas kernels, window_shards(): pl.pallas_call(hand_over, out_shape=tuple((jax.ShapeDtypeStruct(result.sh...  10.1 us

profile of v3, /device:TPU:0, one launch (start us, length us, event | category | flops | bytes accessed | tf_op | source)
XLA Modules:
  0.0 36.1 jit_solution(876276565615000907)
XLA Ops:
  0.6 25.4 %shard_map.130 = (bf16[1024,128]{1,0:T(8,128)(2,1)}, f32[4,8,128]{2,1,0:T(8,128)}, f32[4,8,128]{2,1,0:T(8,128)}) custom-call(s32[4,8,128]{2,1,0:T(8,128)} %refs_0_.1, f32[32]{0:T(128)} %refs_1_.1, f32[4,8,128]{2,1,0:T(8,128)} %refs_2_.1, f32[4,8,128]{2,1,0:T(8,128)} %refs_3_.1, f32[4,8,128]{2,1,0:T(8,128)} %refs_4_.1, f32[4,8,128]{2,1,0:T(8,128)} %refs_5_.1, ...), custom_call_target="tpu_custom_call" | custom-call | tf_op jit(solution)/shard_map/pallas_call | solution.py:607
  26.1 10.1 %shard_map.131 = (bf16[1024,128]{1,0:T(8,128)(2,1)}, f32[4,8,128]{2,1,0:T(8,128)}, f32[4,8,128]{2,1,0:T(8,128)}) custom-call(bf16[1024,128]{1,0:T(8,128)(2,1)} %get-tuple-element.9.refs_0_, f32[4,8,128]{2,1,0:T(8,128)} %get-tuple-element.10.refs_1_, f32[4,8,128]{2,1,0:T(8,128)} %get-tuple-element.11.refs_2_), custom_call_target="tpu_custom_call" | custom-call | tf_op jit(solution)/shard_map/pallas_call | solution.py:645

commit v4 on v3

--- a/solution.py
+++ b/solution.py
@@ -12,6 +12,7 @@
 HALO = 4
 WINDOW_CELLS = 1 << 17
 MESH = pl.DeviceIdType.MESH
+LAYERS = 4
 WIRE = jnp.bfloat16
 VMEM_GRANT = 64 * 1024 * 1024
 
@@ -216,7 +217,6 @@
         field_b,
         speed_ref,
         split_ref,
-        inline_ref,
         base_ref,
         inject_ref,
         stage_ref,
@@ -489,11 +489,14 @@
 
     def advance(tick, state, older):
         weights = jnp.concatenate([base_ref[2 * cols : 3 * cols], inject_ref[tick]], axis=0)
-        inline_ref[...] = jnp.dot(
-            split_ref[:, 0 : 2 * cols], base_ref[0 : 2 * cols], preferred_element_type=f32
-        ) + jnp.dot(split_ref[:, cols : 3 * cols], weights, preferred_element_type=f32)
         for z_at in range(full_z):
-            total = inline_ref[z_at * full_y : (z_at + 1) * full_y]
+            within = z_at % LAYERS
+            if within == 0:
+                part = pl.ds(z_at * full_y, min(LAYERS, full_z - z_at) * full_y)
+                inline = jnp.dot(
+                    split_ref[part, 0 : 2 * cols], base_ref[0 : 2 * cols], preferred_element_type=f32
+                ) + jnp.dot(split_ref[part, cols : 3 * cols], weights, preferred_element_type=f32)
+            total = inline[within * full_y : (within + 1) * full_y]
             z_in = HALO + z_at
             centre = state[z_in, y0 : y0 + full_y, :]
             for distance in range(1, 5):
@@ -584,10 +587,16 @@
 
 
 def hand_over(*refs):
-    copies = [pltpu.make_async_copy(refs[at], refs[3 + at], refs[6].at[at]) for at in range(3)]
-    for copy in copies:
+    given, kept, held = refs[:3], refs[3:6], refs[6:9]
+    first, last = refs[9:]
+    arrive = [pltpu.make_async_copy(given[at], held[at], first.at[at]) for at in range(3)]
+    leave = [pltpu.make_async_copy(held[at], kept[at], last.at[at]) for at in range(3)]
+    for copy in arrive:
         copy.start()
-    for copy in copies:
+    for at in (1, 2, 0):
+        arrive[at].wait()
+        leave[at].start()
+    for copy in leave:
         copy.wait()
 
 
@@ -621,7 +630,6 @@
             pltpu.VMEM(padded, f32),
             pltpu.VMEM((full_z, full_y, cols), f32),
             pltpu.VMEM((full_z * full_y, 3 * cols), bf16),
-            pltpu.VMEM((full_z * full_y, cols), f32),
             pltpu.VMEM((3 * cols, cols), bf16),
             pltpu.VMEM((steps, cols, cols), bf16),
             pltpu.VMEM((IMAGES, depth + 2, rows, cols), f32),
@@ -647,7 +655,8 @@
         out_shape=tuple(jax.ShapeDtypeStruct(result.shape, result.dtype) for result in results),
         in_specs=[hbm] * 3,
         out_specs=(hbm, hbm, hbm),
-        scratch_shapes=[pltpu.SemaphoreType.DMA((3,))],
+        scratch_shapes=[pltpu.VMEM(result.shape, result.dtype) for result in results]
+        + [pltpu.SemaphoreType.DMA((3,)), pltpu.SemaphoreType.DMA((3,))],
         compiler_params=pltpu.CompilerParams(vmem_limit_bytes=VMEM_GRANT),
     )(*results)
     return image.reshape(lag_count, depth, rows, cols), source, receiver

time: 36.4 us -> 28.8 us (0.79)
  Pallas kernels: 35.5 us -> 27.9 us
    pallas_call x1, Pallas kernels: 10.1 us -> 1.71 us  [window_shards(): pl.pallas_call(hand_over, out_shape=tuple((jax.ShapeDtypeStruct(result.sh...]
    pallas_call x1, Pallas kernels: 25.4 us -> 26.2 us  [window_shards(): pl.pallas_call(functools.partial(window_kernel, bands, roles), out_shape=...]
where the time goes in v4:
time: 28.8 us; the launch traced here: 28.5 us
  Pallas kernels  27.9 us (97%)
  between operations  0.64 us (2%)
    pallas_call x1, Pallas kernels, window_shards(): pl.pallas_call(functools.partial(window_kernel, bands, roles), out_shape=...  26.2 us
    pallas_call x1, Pallas kernels, window_shards(): pl.pallas_call(hand_over, out_shape=tuple((jax.ShapeDtypeStruct(result.sh...  1.71 us

profile of v4, /device:TPU:0, one launch (start us, length us, event | category | flops | bytes accessed | tf_op | source)
XLA Modules:
  0.0 28.5 jit_solution(14377480806712409867)
XLA Ops:
  0.6 26.2 %shard_map.130 = (bf16[1024,128]{1,0:T(8,128)(2,1)}, f32[4,8,128]{2,1,0:T(8,128)}, f32[4,8,128]{2,1,0:T(8,128)}) custom-call(s32[4,8,128]{2,1,0:T(8,128)} %refs_0_.1, f32[32]{0:T(128)} %refs_1_.1, f32[4,8,128]{2,1,0:T(8,128)} %refs_2_.1, f32[4,8,128]{2,1,0:T(8,128)} %refs_3_.1, f32[4,8,128]{2,1,0:T(8,128)} %refs_4_.1, f32[4,8,128]{2,1,0:T(8,128)} %refs_5_.1, ...), custom_call_target="tpu_custom_call" | custom-call | tf_op jit(solution)/shard_map/pallas_call | solution.py:616
  26.8 1.7 %shard_map.131 = (bf16[1024,128]{1,0:T(8,128)(2,1)}, f32[4,8,128]{2,1,0:T(8,128)}, f32[4,8,128]{2,1,0:T(8,128)}) custom-call(bf16[1024,128]{1,0:T(8,128)(2,1)} %get-tuple-element.9.refs_0_, f32[4,8,128]{2,1,0:T(8,128)} %get-tuple-element.10.refs_1_, f32[4,8,128]{2,1,0:T(8,128)} %get-tuple-element.11.refs_2_), custom_call_target="tpu_custom_call" | custom-call | tf_op jit(solution)/shard_map/pallas_call | solution.py:653

commit v5 on v4

--- a/solution.py
+++ b/solution.py
@@ -12,7 +12,7 @@
 HALO = 4
 WINDOW_CELLS = 1 << 17
 MESH = pl.DeviceIdType.MESH
-LAYERS = 4
+STRIP = 16
 WIRE = jnp.bfloat16
 VMEM_GRANT = 64 * 1024 * 1024
 
@@ -228,6 +228,7 @@
         snap_recv,
         lend_ref,
         image_buf,
+        early_ref,
         out_sem,
         in_sem,
         lend_send,
@@ -348,7 +349,9 @@
         lane = lax.broadcasted_iota(jnp.int32, (1, cols), 1)
         lane = jnp.where(lane >= half, lane - half, lane)
         for source in range(count):
-            line = src_pos_ref[source, 0] * full_y + src_pos_ref[source, 1]
+            y_at = src_pos_ref[source, 1]
+            strip = lax.div(y_at, STRIP)
+            line = (strip * full_z + src_pos_ref[source, 0]) * STRIP + y_at - strip * STRIP
             target = jnp.where(lane == source, line, target)
         split_ref[:, 2 * cols : 3 * cols] = jnp.where(row_at == target, 1.0, 0.0).astype(jnp.bfloat16)
         height = -(-count // 16) * 16
@@ -372,9 +375,11 @@
 
     @pl.when(core == 1)
     def _():
-        split_ref[:, 2 * cols : 3 * cols] = jnp.where(
-            (row_at < full_y) & (row_at == lane_low), 1.0, 0.0
-        ).astype(jnp.bfloat16)
+        split_ref[:, 2 * cols : 3 * cols] = jnp.zeros((lines, cols), jnp.bfloat16)
+        for strip in range(full_y // STRIP):
+            same = row_at[0:STRIP] + strip * STRIP == lane_low[0:STRIP]
+            top = pl.ds(strip * full_z * STRIP, STRIP)
+            split_ref[top, 2 * cols : 3 * cols] = jnp.where(same, 1.0, 0.0).astype(jnp.bfloat16)
 
     share = steps // 2
     first = pl.multiple_of(share * (1 - core), share)
@@ -479,36 +484,43 @@
     field_a[own_z, own_y, :] = jnp.where(core == 0, src_now_ref[...], rec_now_ref[...])
     field_b[own_z, own_y, :] = jnp.where(core == 0, src_prev_ref[...], rec_prev_ref[...])
 
-    def store_split(z_at, value):
+    def store_split(strip, z_at, value):
         high, low = split_two(value)
-        split_ref[pl.ds(z_at * full_y, full_y), 0:cols] = low
-        split_ref[pl.ds(z_at * full_y, full_y), cols : 2 * cols] = high
-
-    for z_at in range(full_z):
-        store_split(z_at, field_a[HALO + z_at, y0 : y0 + full_y, :])
+        line = pl.ds((strip * full_z + z_at) * STRIP, STRIP)
+        split_ref[line, 0:cols] = low
+        split_ref[line, cols : 2 * cols] = high
+
+    for strip in range(full_y // STRIP):
+        for z_at in range(full_z):
+            at = y0 + strip * STRIP
+            store_split(strip, z_at, field_a[HALO + z_at, at : at + STRIP, :])
 
     def advance(tick, state, older):
         weights = jnp.concatenate([base_ref[2 * cols : 3 * cols], inject_ref[tick]], axis=0)
-        for z_at in range(full_z):
-            within = z_at % LAYERS
-            if within == 0:
-                part = pl.ds(z_at * full_y, min(LAYERS, full_z - z_at) * full_y)
-                inline = jnp.dot(
-                    split_ref[part, 0 : 2 * cols], base_ref[0 : 2 * cols], preferred_element_type=f32
-                ) + jnp.dot(split_ref[part, cols : 3 * cols], weights, preferred_element_type=f32)
-            total = inline[within * full_y : (within + 1) * full_y]
-            z_in = HALO + z_at
-            centre = state[z_in, y0 : y0 + full_y, :]
-            for distance in range(1, 5):
-                pairs = state[z_in - distance, y0 : y0 + full_y, :] + state[z_in + distance, y0 : y0 + full_y, :]
-                pairs = pairs + (
-                    state[z_in, y0 - distance : y0 - distance + full_y, :]
-                    + state[z_in, y0 + distance : y0 + distance + full_y, :]
+        for strip in range(full_y // STRIP):
+            at = y0 + strip * STRIP
+            part = pl.ds(strip * full_z * STRIP, full_z * STRIP)
+            inline = jnp.dot(
+                split_ref[part, 0 : 2 * cols], base_ref[0 : 2 * cols], preferred_element_type=f32
+            ) + jnp.dot(split_ref[part, cols : 3 * cols], weights, preferred_element_type=f32)
+            layers = [state[HALO + z_at, at : at + STRIP, :] for z_at in range(full_z)]
+            for z_at in range(full_z):
+                total = inline[z_at * STRIP : (z_at + 1) * STRIP]
+                z_in = HALO + z_at
+                for distance in range(1, 5):
+                    pairs = (
+                        state[z_in, at - distance : at - distance + STRIP, :]
+                        + state[z_in, at + distance : at + distance + STRIP, :]
+                    )
+                    for other in (z_at - distance, z_at + distance):
+                        if 0 <= other < full_z:
+                            pairs = pairs + layers[other]
+                    total = total + STENCIL_WEIGHTS[distance] * pairs
+                updated = (2.0 * layers[z_at] - older[z_in, at : at + STRIP, :]) + (
+                    speed_ref[z_at, strip * STRIP : (strip + 1) * STRIP] * total
                 )
-                total = total + STENCIL_WEIGHTS[distance] * pairs
-            updated = (2.0 * centre - older[z_in, y0 : y0 + full_y, :]) + speed_ref[z_at] * total
-            older[z_in, y0 : y0 + full_y, :] = updated
-            store_split(z_at, updated)
+                older[z_in, at : at + STRIP, :] = updated
+                store_split(strip, z_at, updated)
 
     partner_role = 2 * column + 1 - core
     deep = depth + 2
@@ -538,8 +550,26 @@
         return carry
 
     lax.fori_loop(0, IMAGES, one_image, 0)
-    for snapshot in range(IMAGES):
+    def correlate(slot, snapshots, summed):
+        lag = lags_ref[slot]
+        back = jnp.where(lag > 0, cols - 2 * lag, -2 * lag)
+        for snapshot in snapshots:
+            moved = pltpu.roll(snap_ref[snapshot, 1].reshape(deep * rows, cols), back, 1)
+            summed = summed + snap_ref[snapshot, 0].reshape(deep * rows, cols) * moved
+        return summed
+
+    lag_count = lags_ref.shape[0]
+    group = -(-lag_count // 4)
+    last = IMAGES - 1
+    for snapshot in range(last):
         snap_copy(snapshot).wait()
+
+    def early_lag(slot, carry):
+        early_ref[slot] = correlate(slot, range(last), jnp.zeros((deep * rows, cols), f32))
+        return carry
+
+    lax.fori_loop(0, lag_count, early_lag, 0, unroll=group)
+    snap_copy(last).wait()
     results = [
         pltpu.make_async_copy(snap_ref.at[IMAGES - 1, side, pl.ds(1, depth)], kept, out_sem.at[side])
         for side, kept in enumerate((src_out_ref, rec_out_ref))
@@ -549,12 +579,8 @@
 
     def one_lag(slot, carry):
         lag = lags_ref[slot]
-        back = jnp.where(lag > 0, cols - 2 * lag, -2 * lag)
         shift = jnp.where(lag < 0, cols + lag, lag)
-        summed = jnp.zeros((deep * rows, cols), f32)
-        for snapshot in range(IMAGES):
-            moved = pltpu.roll(snap_ref[snapshot, 1].reshape(deep * rows, cols), back, 1)
-            summed = summed + snap_ref[snapshot, 0].reshape(deep * rows, cols) * moved
+        summed = correlate(slot, (last,), early_ref[slot])
         filtered = (
             2.0 * summed[rows : rows + cells] - summed[0:cells] - summed[2 * rows : 2 * rows + cells]
         )
@@ -566,8 +592,6 @@
         image_buf[pl.ds(at, cells)] = jnp.where(inside, filtered, 0.0).astype(jnp.bfloat16)
         return carry
 
-    lag_count = lags_ref.shape[0]
-    group = -(-lag_count // 4)
     for turn, start in enumerate(range(0, lag_count, group)):
         stop = min(start + group, lag_count)
         lax.fori_loop(start, stop, one_lag, 0, unroll=group)
@@ -641,6 +665,7 @@
             pltpu.SemaphoreType.DMA((IMAGES,)),
             pltpu.VMEM((2, steps // 2, full_y, cols), bf16),
             pltpu.VMEM((lag_count * cells, cols), bf16),
+            pltpu.VMEM((lag_count, cells + 2 * rows, cols), f32),
             pltpu.SemaphoreType.DMA((6,)),
             pltpu.SemaphoreType.DMA((len(arrays),)),
             pltpu.SemaphoreType.DMA((2,)),
@@ -668,7 +693,7 @@
     small = depth * roles * rows * bands * cols <= WINDOW_CELLS
     fits = roles % 2 == 0 and rows % 8 == 0 and cols % 128 == 0
     fits = fits and max(rows * bands, sources) <= cols // 2 and arrays[10].shape[0] < cols
-    fits = fits and (depth * rows) % 16 == 0 and arrays[1].shape[0] <= 256
+    fits = fits and (depth * rows) % 16 == 0 and (rows * bands) % STRIP == 0 and arrays[1].shape[0] <= 256
     if small and fits:
         return window_shards(bands, roles, *arrays)
     return tile_shards(*arrays)

time: 28.8 us -> 26.9 us (0.934)
  Pallas kernels: 27.9 us -> 26 us
    pallas_call x1, Pallas kernels: 26.2 us -> 24.3 us  [window_shards(): pl.pallas_call(functools.partial(window_kernel, bands, roles), out_shape=...]
where the time goes in v5:
time: 26.9 us; the launch traced here: 26.6 us
  Pallas kernels  26 us (97%)
  between operations  0.64 us (2%)
    pallas_call x1, Pallas kernels, window_shards(): pl.pallas_call(functools.partial(window_kernel, bands, roles), out_shape=...  24.3 us
    pallas_call x1, Pallas kernels, window_shards(): pl.pallas_call(hand_over, out_shape=tuple((jax.ShapeDtypeStruct(result.sh...  1.71 us

profile of v5, /device:TPU:0, one launch (start us, length us, event | category | flops | bytes accessed | tf_op | source)
XLA Modules:
  0.0 26.6 jit_solution(10882406271303851811)
XLA Ops:
  0.6 24.3 %shard_map.130 = (bf16[1024,128]{1,0:T(8,128)(2,1)}, f32[4,8,128]{2,1,0:T(8,128)}, f32[4,8,128]{2,1,0:T(8,128)}) custom-call(s32[4,8,128]{2,1,0:T(8,128)} %refs_0_.1, f32[32]{0:T(128)} %refs_1_.1, f32[4,8,128]{2,1,0:T(8,128)} %refs_2_.1, f32[4,8,128]{2,1,0:T(8,128)} %refs_3_.1, f32[4,8,128]{2,1,0:T(8,128)} %refs_4_.1, f32[4,8,128]{2,1,0:T(8,128)} %refs_5_.1, ...), custom_call_target="tpu_custom_call" | custom-call | tf_op jit(solution)/shard_map/pallas_call | solution.py:640
  24.9 1.7 %shard_map.131 = (bf16[1024,128]{1,0:T(8,128)(2,1)}, f32[4,8,128]{2,1,0:T(8,128)}, f32[4,8,128]{2,1,0:T(8,128)}) custom-call(bf16[1024,128]{1,0:T(8,128)(2,1)} %get-tuple-element.9.refs_0_, f32[4,8,128]{2,1,0:T(8,128)} %get-tuple-element.10.refs_1_, f32[4,8,128]{2,1,0:T(8,128)} %get-tuple-element.11.refs_2_), custom_call_target="tpu_custom_call" | custom-call | tf_op jit(solution)/shard_map/pallas_call | solution.py:678

commit v6 on v5

--- a/solution.py
+++ b/solution.py
@@ -333,6 +333,18 @@
     for step in range(1, columns):
         pass_on(step, out_buf.at[core], own, step)
 
+    high, low = split_two(inline_matrix(cols))
+    base_ref[0:cols] = high
+    base_ref[cols : 2 * cols] = high
+    base_ref[2 * cols : 3 * cols] = low
+    field_a[...] = jnp.zeros_like(field_a)
+    field_b[...] = jnp.zeros_like(field_b)
+
+    slot = band * roles + 2 * column + 1 - core
+    landed(slot)
+    for step in range(1, columns):
+        pass_on(step, blocks.at[slot], slot, columns + step)
+
     for at in (1, 6, 7, 8, 9, 10):
         fetches[at].wait()
     lines = split_ref.shape[0]
@@ -366,13 +378,6 @@
             inject_ref[tick, 0:height] = high
             inject_ref[tick, half : half + height] = low
 
-    high, low = split_two(inline_matrix(cols))
-    base_ref[0:cols] = high
-    base_ref[cols : 2 * cols] = high
-    base_ref[2 * cols : 3 * cols] = low
-    field_a[...] = jnp.zeros_like(field_a)
-    field_b[...] = jnp.zeros_like(field_b)
-
     @pl.when(core == 1)
     def _():
         split_ref[:, 2 * cols : 3 * cols] = jnp.zeros((lines, cols), jnp.bfloat16)
@@ -408,20 +413,16 @@
             )
         return total
 
-    middle = count // 2 // chunk * chunk
-    added = add_receivers(jnp.zeros((2 * share * full_y, cols), f32), 0, middle)
-
-    slot = band * roles + 2 * column + 1 - core
-    landed(slot)
-    for step in range(1, columns):
-        pass_on(step, blocks.at[slot], slot, columns + step)
+    chunks = -(-count // chunk)
+    stops = [min(count, chunk * (-(-chunks * (hop + 1) // bands))) for hop in range(bands)]
+    added = add_receivers(jnp.zeros((2 * share * full_y, cols), f32), 0, stops[0])
     for hop in range(1, bands):
         for side in range(2):
             slot = lax.rem(band + hop, bands) * roles + 2 * column + side
             landed(slot)
             for step in range(1, columns):
                 pass_on(step, blocks.at[slot], slot, (2 * hop + side) * columns + step)
-    added = add_receivers(added, middle, count)
+        added = add_receivers(added, stops[hop - 1], stops[hop])
     size = share * full_y
     high, low = split_two(added[0:size] + added[size : 2 * size])
     lend_ref[0] = high.reshape(share, full_y, cols)

time: 26.9 us -> 26.9 us (level)
  no operation moved by 1% of the time
where the time goes in v6:
time: 26.9 us; the launch traced here: 26.6 us
  Pallas kernels  26 us (97%)
  between operations  0.64 us (2%)
    pallas_call x1, Pallas kernels, window_shards(): pl.pallas_call(functools.partial(window_kernel, bands, roles), out_shape=...  24.3 us
    pallas_call x1, Pallas kernels, window_shards(): pl.pallas_call(hand_over, out_shape=tuple((jax.ShapeDtypeStruct(result.sh...  1.71 us

profile of v6, /device:TPU:0, one launch (start us, length us, event | category | flops | bytes accessed | tf_op | source)
XLA Modules:
  0.0 26.6 jit_solution(8118134663384132062)
XLA Ops:
  0.6 24.3 %shard_map.130 = (bf16[1024,128]{1,0:T(8,128)(2,1)}, f32[4,8,128]{2,1,0:T(8,128)}, f32[4,8,128]{2,1,0:T(8,128)}) custom-call(s32[4,8,128]{2,1,0:T(8,128)} %refs_0_.1, f32[32]{0:T(128)} %refs_1_.1, f32[4,8,128]{2,1,0:T(8,128)} %refs_2_.1, f32[4,8,128]{2,1,0:T(8,128)} %refs_3_.1, f32[4,8,128]{2,1,0:T(8,128)} %refs_4_.1, f32[4,8,128]{2,1,0:T(8,128)} %refs_5_.1, ...), custom_call_target="tpu_custom_call" | custom-call | tf_op jit(solution)/shard_map/pallas_call | solution.py:641
  24.9 1.7 %shard_map.131 = (bf16[1024,128]{1,0:T(8,128)(2,1)}, f32[4,8,128]{2,1,0:T(8,128)}, f32[4,8,128]{2,1,0:T(8,128)}) custom-call(bf16[1024,128]{1,0:T(8,128)(2,1)} %get-tuple-element.9.refs_0_, f32[4,8,128]{2,1,0:T(8,128)} %get-tuple-element.10.refs_1_, f32[4,8,128]{2,1,0:T(8,128)} %get-tuple-element.11.refs_2_), custom_call_target="tpu_custom_call" | custom-call | tf_op jit(solution)/shard_map/pallas_call | solution.py:679

commit v7 on v6

--- a/solution.py
+++ b/solution.py
@@ -401,10 +401,15 @@
             in_col = jnp.where(in_col, 1.0, 0.0).astype(jnp.bfloat16)
             amounts = rec_trace_ref[pl.ds(first, share), at : at + size]
             high = amounts.astype(jnp.bfloat16).astype(f32)
+            masks = [
+                jnp.where(in_row[at_row : at_row + STRIP], 1.0, 0.0).astype(jnp.bfloat16)
+                for at_row in range(0, full_y, STRIP)
+            ]
             parts = []
             for part in (high, amounts - high):
                 for tick in range(share):
-                    parts.append(jnp.where(in_row, part[tick : tick + 1], 0.0).astype(jnp.bfloat16))
+                    line = jnp.broadcast_to(part[tick : tick + 1], (STRIP, size)).astype(jnp.bfloat16)
+                    parts.extend(mask * line for mask in masks)
             total = total + lax.dot_general(
                 jnp.concatenate(parts, axis=0),
                 in_col,

time: 26.9 us -> 26.9 us (level)
  no operation moved by 1% of the time
where the time goes in v7:
time: 26.9 us; the launch traced here: 26.6 us
  Pallas kernels  26 us (97%)
  between operations  0.64 us (2%)
    pallas_call x1, Pallas kernels, window_shards(): pl.pallas_call(functools.partial(window_kernel, bands, roles), out_shape=...  24.3 us
    pallas_call x1, Pallas kernels, window_shards(): pl.pallas_call(hand_over, out_shape=tuple((jax.ShapeDtypeStruct(result.sh...  1.71 us

profile of v7, /device:TPU:0, one launch (start us, length us, event | category | flops | bytes accessed | tf_op | source)
XLA Modules:
  0.0 26.6 jit_solution(14147057653454024662)
XLA Ops:
  0.6 24.3 %shard_map.130 = (bf16[1024,128]{1,0:T(8,128)(2,1)}, f32[4,8,128]{2,1,0:T(8,128)}, f32[4,8,128]{2,1,0:T(8,128)}) custom-call(s32[4,8,128]{2,1,0:T(8,128)} %refs_0_.1, f32[32]{0:T(128)} %refs_1_.1, f32[4,8,128]{2,1,0:T(8,128)} %refs_2_.1, f32[4,8,128]{2,1,0:T(8,128)} %refs_3_.1, f32[4,8,128]{2,1,0:T(8,128)} %refs_4_.1, f32[4,8,128]{2,1,0:T(8,128)} %refs_5_.1, ...), custom_call_target="tpu_custom_call" | custom-call | tf_op jit(solution)/shard_map/pallas_call | solution.py:646
  24.9 1.7 %shard_map.131 = (bf16[1024,128]{1,0:T(8,128)(2,1)}, f32[4,8,128]{2,1,0:T(8,128)}, f32[4,8,128]{2,1,0:T(8,128)}) custom-call(bf16[1024,128]{1,0:T(8,128)(2,1)} %get-tuple-element.9.refs_0_, f32[4,8,128]{2,1,0:T(8,128)} %get-tuple-element.10.refs_1_, f32[4,8,128]{2,1,0:T(8,128)} %get-tuple-element.11.refs_2_), custom_call_target="tpu_custom_call" | custom-call | tf_op jit(solution)/shard_map/pallas_call | solution.py:684
